TPU v7x, 32 devices: a whole 2x2x4 slice. The times are simulated.
32 devices in a mesh: dp: 8 (over y, x, core), fsdp: 4 (over z).
Axes of the slice: x: 2, y: 2, z: 4, core: 2. Of those that a mesh axis runs over, the one named last changes fastest.
Arguments:
- hidden: bfloat16 [12288, 5120], P(('dp', 'fsdp')), may hold values from -6 to 6
- norm_gain: bfloat16 [5120], replicated, may hold values from 0.25 to 1.75
- q_weight: bfloat16 [5120, 2560], P('dp', 'fsdp')
- kv_weight: bfloat16 [5120, 1024], P('dp', 'fsdp')
- q_bias: bfloat16 [2560], replicated, may hold values from -3 to 3
- kv_bias: bfloat16 [1024], replicated, may hold values from -3 to 3
- segments: int32 [12288], P(('dp', 'fsdp')), may hold values from -1 to 383, as said below
Outputs:
- attention_context: bfloat16 [12288, 2560], P(('dp', 'fsdp'))
Inputs may be any that keep to these rules, and one draw needn't show every extreme that they name: `segments`: in each device's run of 384 rows the live rows are its first whole blocks of 128; their ids start at 0 and never fall, each rollout has 1 to 256 rows, and somewhere in the slice one rollout has exactly 256; the other rows are -1. The devices at dp indices i and i + 8 / 2 with the same fsdp index hold exactly 4 live blocks together, and some device holds 3. Some device has 384 rollouts of one row each.
All inputs are finite; a program needn't handle non-finite values.
Results may differ from a plain program's by a relative error of at most 0.0058.
Values may be sent and summed in bfloat16 or wider, within the bound.
A program may use at most 128 MiB of HBM per device.

v0:
```python
import jax
import jax.numpy as jnp
from jax import lax
from jax.sharding import PartitionSpec as P

HEADS = 20
KV_HEADS = 4
HEAD_DIM = 128
BLOCK = 128


def positions_of(segments):
    row_ids = jnp.arange(segments.shape[0], dtype=jnp.int32)
    before = jnp.concatenate([jnp.full((1,), -3, jnp.int32), segments[:-1]])
    starts = jnp.where(segments != before, row_ids, 0)
    return row_ids - lax.cummax(starts, axis=0)


def rotate(source, positions):
    half_dim = HEAD_DIM // 2
    frequency = jnp.exp(
        jnp.arange(half_dim, dtype=jnp.float32)
        * (-2.0 / HEAD_DIM)
        * jnp.log(jnp.float32(1000000.0))
    )
    angles = positions.astype(jnp.float32)[:, None] * frequency[None, :]
    cosine = jnp.cos(angles)[:, None, :]
    sine_part = jnp.sin(angles)[:, None, :]
    lower_half = source[..., :half_dim]
    second = source[..., half_dim:]
    return jnp.concatenate(
        [lower_half * cosine - second * sine_part, second * cosine + lower_half * sine_part],
        axis=-1,
    )


def normalize(hidden, norm_gain):
    as_float = hidden.astype(jnp.float32)
    mean_square = jnp.mean(as_float * as_float, axis=-1, keepdims=True)
    return (as_float * lax.rsqrt(mean_square + 1e-06) * norm_gain.astype(jnp.float32)).astype(
        jnp.bfloat16
    )


def windows(source, fill_value):
    block_count = source.shape[0] // BLOCK
    shaped = source.reshape((block_count, BLOCK) + source.shape[1:])
    padded = jnp.concatenate(
        [jnp.full((2,) + shaped.shape[1:], fill_value, source.dtype), shaped], axis=0
    )
    return jnp.concatenate(
        [padded[0:block_count], padded[1 : block_count + 1], padded[2 : block_count + 2]], axis=1
    )


def attend(queries, key_rows, values, segments):
    row_count = queries.shape[0]
    block_count = row_count // BLOCK
    group_size = HEADS // KV_HEADS
    row_ids = jnp.arange(row_count, dtype=jnp.int32)
    key_win = windows(key_rows, 0)
    value_win = windows(values, 0)
    seg_win = windows(segments, -2)
    row_win = windows(row_ids, -1)
    q_blocks = queries.reshape(block_count, BLOCK, KV_HEADS, group_size, HEAD_DIM)
    scores = jnp.einsum(
        "bqkgd,bskd->bkgqs", q_blocks, key_win, preferred_element_type=jnp.float32
    ) * HEAD_DIM ** (-0.5)
    q_seg = segments.reshape(block_count, BLOCK)
    q_row = row_ids.reshape(block_count, BLOCK)
    allowed = (
        (seg_win[:, None, :] == q_seg[:, :, None])
        & (row_win[:, None, :] <= q_row[:, :, None])
        & (q_seg[:, :, None] >= 0)
    )
    scores = jnp.where(allowed[:, None, None], scores, -1e30)
    row_max = jnp.max(scores, axis=-1, keepdims=True)
    exponents = jnp.exp(scores - row_max)
    probabilities = (exponents / jnp.sum(exponents, axis=-1, keepdims=True)).astype(jnp.bfloat16)
    context = jnp.einsum(
        "bkgqs,bskd->bqkgd", probabilities, value_win, preferred_element_type=jnp.float32
    )
    context = jnp.where((q_seg >= 0)[:, :, None, None, None], context, 0.0)
    return context.reshape(row_count, HEADS * HEAD_DIM).astype(jnp.bfloat16)


def project(row_input, positions, q_weight, kv_weight, q_bias, kv_bias):
    row_count = row_input.shape[0]
    q_rows_full, kv_rows_full = (
        lax.all_gather(q_weight, "fsdp", axis=1, tiled=True),
        lax.all_gather(kv_weight, "fsdp", axis=1, tiled=True),
    )

    def add_rows(piece_rows):
        return jnp.dot(row_input, piece_rows, preferred_element_type=jnp.float32)

    q_lin = add_rows(lax.all_gather(q_rows_full, "dp", axis=0, tiled=True))
    kv_lin = add_rows(lax.all_gather(kv_rows_full, "dp", axis=0, tiled=True))
    q_lin = q_lin + q_bias.astype(jnp.float32)
    kv_lin = kv_lin + kv_bias.astype(jnp.float32)
    split_at = KV_HEADS * HEAD_DIM
    queries = rotate(q_lin.reshape(row_count, HEADS, HEAD_DIM), positions).astype(jnp.bfloat16)
    key_rows = rotate(
        kv_lin[:, :split_at].reshape(row_count, KV_HEADS, HEAD_DIM), positions
    ).astype(jnp.bfloat16)
    values = kv_lin[:, split_at:].reshape(row_count, KV_HEADS, HEAD_DIM).astype(jnp.bfloat16)
    return (queries, key_rows, values)


def local(hidden, norm_gain, q_weight, kv_weight, q_bias, kv_bias, segments):
    normed = normalize(hidden, norm_gain)
    positions = positions_of(segments)
    queries, key_rows, values = project(normed, positions, q_weight, kv_weight, q_bias, kv_bias)
    return attend(queries, key_rows, values, segments)


def solution(mesh):
    in_specs = (
        P(("dp", "fsdp"), None),
        P(),
        P("dp", "fsdp"),
        P("dp", "fsdp"),
        P(),
        P(),
        P(("dp", "fsdp")),
    )
    out_specs = P(("dp", "fsdp"), None)
    return jax.shard_map(local, mesh=mesh, in_specs=in_specs, out_specs=out_specs, check_vma=False)
```

profile of v0, /device:TPU:0, one launch (start us, length us, event | category | flops | bytes accessed | tf_op | source)
XLA Modules:
  0.0 385.5 jit_solution(11633247205806317430)
XLA Ops:
  6.6 0.7 all-gather.5.cloned.1.call-update
  7.3 0.7 all-gather.9.cloned.1.call-update
  8.1 37.0 %all-gather.5.cloned.1.call-done = bf16[640,1024]{1,0:T(8,128)(2,1)} async-done(((bf16[640,256]{1,0:T(8,128)(2,1)}), bf16[640,1024]{1,0:T(8,128)(2,1)}) %all-gather.5.cloned.1.call-update) | async-done | bytes 1310736 | tf_op jit(solution)/shard_map/all_gather | solution.py:91
  45.2 65.6 %all-gather.9.cloned.1.call-done = bf16[640,2560]{1,0:T(8,128)(2,1)} async-done(((bf16[640,640]{1,0:T(8,128)(2,1)}), bf16[640,2560]{1,0:T(8,128)(2,1)}) %all-gather.9.cloned.1.call-update) | async-done | bytes 3276816 | tf_op jit(solution)/shard_map/all_gather | solution.py:90
  111.0 0.3 reduce-window.9
  111.6 3.0 fusion.2
  114.6 0.5 and_and_fusion
  115.1 0.4 multiply_cosine_fusion
  115.6 59.2 %all-gather.7.cloned.1.call-done = bf16[5120,1024]{1,0:T(8,128)(2,1)} async-done(((bf16[640,1024]{1,0:T(8,128)(2,1)}), bf16[5120,1024]{1,0:T(8,128)(2,1)}) %all-gather.7.cloned.1.call-update) | async-done | bytes 10485776 | tf_op jit(solution)/shard_map/all_gather | solution.py:98
  174.7 8.2 %convolution_add_fusion.1 = f32[384,1024]{1,0:T(8,128)S(1)} fusion(bf16[5120,1024]{1,0:T(8,128)(2,1)} %all-gather.7.cloned.1.call-done, bf16[384,5120]{1,0:T(8,128)(2,1)} %param.7, f32[5120]{0:T(1024)S(1)} %convert_element_type.45, f32[384]{0:T(512)S(1)} %add_rsqrt_fusion, f32[1024]{0:T(1024)S(1)} %convert_element_type.47), kind=kOutput, calls=%fused_computation.23 | convolution fusion | flops 4034789376 | bytes 16016896 | tf_op jit(solution)/shard_map/dot_general | solution.py:95
  184.8 1.0 pad_slice_fusion.1
  185.8 1.0 fusion.34
  186.8 119.4 %all-gather.11.cloned.1.call-done = bf16[5120,2560]{1,0:T(8,128)(2,1)} async-done(((bf16[640,2560]{1,0:T(8,128)(2,1)}), bf16[5120,2560]{1,0:T(8,128)(2,1)}) %all-gather.11.cloned.1.call-update) | async-done | bytes 26214416 | tf_op jit(solution)/shard_map/all_gather | solution.py:97
  306.3 17.8 %convolution_add_fusion = f32[384,2560]{1,0:T(8,128)} fusion(bf16[5120,2560]{1,0:T(8,128)(2,1)} %all-gather.11.cloned.1.call-done, f32[2560]{0:T(1024)S(1)} %convert_element_type.50, bf16[384,5120]{1,0:T(8,128)(2,1)} %param.7, f32[5120]{0:T(1024)S(1)} %convert_element_type.45, f32[384]{0:T(512)S(1)} %add_rsqrt_fusion), kind=kOutput, calls=%fused_computation.14 | convolution fusion | flops 10075176960 | bytes 34110976 | tf_op jit(solution)/shard_map/dot_general | solution.py:95
  324.1 5.5 %copy.17 = f32[384,2560]{0,1:T(8,128)} copy(f32[384,2560]{1,0:T(8,128)} %convolution_add_fusion) | data formatting | bytes 7864320 | tf_op jit(solution)/shard_map/add | solution.py:99
  329.6 3.7 subtract_convert_fusion
  333.5 1.4 copy.19
  334.9 2.7 concatenate.57
  337.6 2.4 copy.18
  340.0 8.2 %fusion.10 = f32[3,4,384,128,5]{3,2,4,1,0:T(8,128)} fusion(bf16[3,128,4,5,64]{4,1,3,2,0:T(8,128)(2,1)S(1)} %copy.19, bf16[3,128,4,5,64]{4,1,3,2,0:T(8,128)(2,1)} %copy.18, bf16[3,128,4,64]{3,1,2,0:T(8,128)(2,1)} %copy-done, bf16[3,128,4,64]{3,1,2,0:T(8,128)(2,1)} %copy-done.1, bf16[3,128,4,128]{3,1,2,0:T(8,128)(2,1)} %get-tuple-element.10, ...), kind=kOutput, calls=%fused_computation.17 | convolution fusion | flops 763625472 | bytes 14942208 | tf_op jit(solution)/shard_map/bqkgd,bskd->bkgqs/dot_general | solution.py:66
  348.2 16.9 %fusion.35 = (f32[3,4,5,128]{3,2,1,0:T(8,128)S(1)}, f32[3,4,5,128,384]{3,4,2,1,0:T(8,128)}) fusion(f32[3,4,384,128,5]{3,2,4,1,0:T(8,128)} %fusion.10, pred[3,128,384]{1,2,0:T(8,128)(4,1)S(1)} %and_and_fusion), kind=kOutput, calls=%fused_computation.68 | output fusion | flops 17695104 | bytes 23771136 | tf_op jit(solution)/shard_map/sub | solution.py:78
  365.0 7.1 %fusion.9 = bf16[3,128,4,5,128]{1,4,3,2,0:T(8,128)(2,1)} fusion(pred[3,128]{1,0:T(4,128)(4,1)S(1)} %broadcast_compare_fusion, f32[3,4,5,128,384]{3,4,2,1,0:T(8,128)} %get-tuple-element.20, f32[3,4,5,128]{3,2,1,0:T(8,128)S(1)} %get-tuple-element.19, bf16[3,128,4,128]{1,3,2,0:T(8,128)(2,1)S(1)} %copy-done.3, bf16[3,128,4,128]{1,3,2,0:T(8,128)(2,1)S(1)} %copy-done.5, ...), kind=kOutput, calls=%fused_computation.16 | convolution fusion | flops 766377984 | bytes 14973312 | tf_op jit(solution)/shard_map/bkgqs,bskd->bqkgd/dot_general | solution.py:80
  372.2 3.6 copy.26
  375.8 3.2 reshape.173
  (53 shorter events, 2.7 us)
Async XLA Ops:
  6.5 104.3 %copy-start.8 = (bf16[2560]{0:T(1024)(128)(2,1)S(1)}, bf16[2560]{0:T(1024)(128)(2,1)}, u32[]{:S(2)}) copy-start(bf16[2560]{0:T(1024)(128)(2,1)} %param.11) | copy-start | bytes 15364
  6.5 104.3 %copy-start.7 = (bf16[5120]{0:T(1024)(128)(2,1)S(1)}, bf16[5120]{0:T(1024)(128)(2,1)}, u32[]{:S(2)}) copy-start(bf16[5120]{0:T(1024)(128)(2,1)} %param.8) | copy-start | bytes 30724
  6.5 104.4 %copy-start.6 = (s32[384]{0:T(512)S(1)}, s32[384]{0:T(512)}, u32[]{:S(2)}) copy-start(s32[384]{0:T(512)} %param.13) | copy-start | bytes 4612
  6.5 104.9 %copy-start.9 = (bf16[1024]{0:T(1024)(128)(2,1)S(1)}, bf16[1024]{0:T(1024)(128)(2,1)}, u32[]{:S(2)}) copy-start(bf16[1024]{0:T(1024)(128)(2,1)} %param.12) | copy-start | bytes 6148
  6.5 38.6 %all-gather.5.cloned.1.call-start = ((), (), s32[]{:S(2)}) async-start(), calls=%async_computation | async-start | bytes 1638400 | tf_op jit(solution)/shard_map/all_gather | solution.py:91
  7.3 103.6 %all-gather.9.cloned.1.call-start = ((), (), s32[]{:S(2)}) async-start(), calls=%async_computation.2 | async-start | bytes 4096000 | tf_op jit(solution)/shard_map/all_gather | solution.py:90
  8.0 166.7 %all-gather.7.cloned.1.call-start = ((), (), s32[]{:S(2)}) async-start(), calls=%async_computation.1 | async-start | bytes 11796480 | tf_op jit(solution)/shard_map/all_gather | solution.py:98
  45.1 261.1 %all-gather.11.cloned.1.call-start = ((), (), s32[]{:S(2)}) async-start(), calls=%async_computation.3 | async-start | bytes 29491200 | tf_op jit(solution)/shard_map/all_gather | solution.py:97
  183.8 140.3 %copy-start = (bf16[3,128,4,64]{3,1,2,0:T(8,128)(2,1)}, bf16[3,128,4,64]{3,1,2,0:T(8,128)(2,1)S(1)}, u32[]{:S(2)}) copy-start(bf16[3,128,4,64]{3,1,2,0:T(8,128)(2,1)S(1)} %copy.16) | copy-start | bytes 589828
  184.1 139.9 %copy-start.1 = (bf16[3,128,4,64]{3,1,2,0:T(8,128)(2,1)}, bf16[3,128,4,64]{3,1,2,0:T(8,128)(2,1)S(1)}, u32[]{:S(2)}) copy-start(bf16[3,128,4,64]{3,1,2,0:T(8,128)(2,1)S(1)} %copy.15) | copy-start | bytes 589828
  184.5 139.6 %copy-start.2 = (bf16[3,128,4,128]{1,3,2,0:T(8,128)(2,1)}, bf16[3,128,4,128]{1,3,2,0:T(8,128)(2,1)S(1)}, u32[]{:S(2)}) copy-start(bf16[3,128,4,128]{1,3,2,0:T(8,128)(2,1)S(1)} %copy.11) | copy-start | bytes 1179652
  348.2 16.9 %copy-start.3 = (bf16[3,128,4,128]{1,3,2,0:T(8,128)(2,1)S(1)}, bf16[3,128,4,128]{1,3,2,0:T(8,128)(2,1)}, u32[]{:S(2)}) copy-start(bf16[3,128,4,128]{1,3,2,0:T(8,128)(2,1)} %copy-done.2) | copy-start | bytes 1179652
  348.2 16.9 %copy-start.4 = (bf16[3,128,4,128]{1,3,2,0:T(8,128)(2,1)S(1)}, bf16[3,128,4,128]{1,3,2,0:T(8,128)(2,1)}, u32[]{:S(2)}) copy-start(bf16[3,128,4,128]{1,3,2,0:T(8,128)(2,1)} %get-tuple-element.11) | copy-start | bytes 1179652
  348.2 16.9 %copy-start.5 = (bf16[3,128,4,128]{1,3,2,0:T(8,128)(2,1)S(1)}, bf16[3,128,4,128]{1,3,2,0:T(8,128)(2,1)}, u32[]{:S(2)}) copy-start(bf16[3,128,4,128]{1,3,2,0:T(8,128)(2,1)} %get-tuple-element.12) | copy-start | bytes 1179652
Sparse Core Ops, SparseCore 0:
  8.9 36.1 all-gather.4
  46.7 64.0 all-gather.8
  112.7 61.9 all-gather.6
  176.5 129.7 all-gather.10
where the time goes:
time: 386 us
  waiting for transfers between devices  283 us (73%)
  matrix products  41.3 us (11%)
  other arithmetic  25.3 us (7%)
  local copies, waits for them, and re-layouts  22.7 us (6%)
  between operations  13.4 us (3%)
    all_gather x1, waiting for transfers between devices, project(): q_lin = add_rows(lax.all_gather(q_rows_full, 'dp', axis=0, tiled=True))  119 us
    all_gather x1, waiting for transfers between devices, project(): lax.all_gather(q_weight, 'fsdp', axis=1, tiled=True)  65.6 us
    all_gather x1, waiting for transfers between devices, project(): kv_lin = add_rows(lax.all_gather(kv_rows_full, 'dp', axis=0, tiled=True))  59.2 us
    all_gather x1, waiting for transfers between devices, project(): lax.all_gather(kv_weight, 'fsdp', axis=1, tiled=True)  37 us
    dot_general x2, matrix products, add_rows(): return jnp.dot(row_input, piece_rows, preferred_element_type=jnp.float32)  26 us
    sub x1, other arithmetic, attend(): exponents = jnp.exp(scores - row_max)  16.9 us
    dot_general x1, matrix products, attend(): jnp.einsum('bqkgd,bskd->bkgqs', q_blocks, key_win, preferred_element_type...  8.2 us
  transfers between devices with their start and end apart: 4, of which 4 were waited for; matrix products, arithmetic and copies ran while one was open for 4% of the time, Pallas kernels for 0%

commit v1 on v0

--- a/solution.py
+++ b/solution.py
@@ -1,12 +1,335 @@
+import functools
+
 import jax
 import jax.numpy as jnp
 from jax import lax
+from jax.experimental import pallas as pl
+from jax.experimental.pallas import tpu as pltpu
 from jax.sharding import PartitionSpec as P
 
 HEADS = 20
 KV_HEADS = 4
 HEAD_DIM = 128
 BLOCK = 128
+LANES = 128
+MESH = pl.DeviceIdType.MESH
+TO_X, TO_Y, TO_UP, TO_DOWN, TO_SIB = range(5)
+OWN, VIA_X, VIA_Y, DIAG = range(4)
+
+
+def gather_project_kernel(
+    ndp, nz, pieces, late,
+    hidden_ref, gain_ref, qw_ref, kvw_ref, qb_ref, kvb_ref, seg_ref,
+    q_out, k_out, v_out,
+    wbuf, raw, normed, acc, cos_t, sin_t, local_sem, send_sem, recv_sem,
+):
+    rows, width = raw.shape
+    depth, qcols = qw_ref.shape
+    kvcols = kvw_ref.shape[1]
+    cols = qcols + kvcols
+    step = depth // pieces
+    me = lax.axis_index("dp")
+    z = lax.axis_index("fsdp")
+    core = lax.rem(me, 2)
+    x = lax.rem(me // 2, 2)
+    y = me // 4
+    sib = me + 1 - 2 * core
+    xn = me + 2 - 4 * x
+    yn = me + 4 - 8 * y
+    dg = xn + yn - me
+    source = [me, xn, yn, dg]
+
+    own_q = pltpu.make_async_copy(qw_ref, wbuf.at[me, z, :, pl.ds(0, qcols)], local_sem.at[0])
+    own_kv = pltpu.make_async_copy(kvw_ref, wbuf.at[me, z, :, pl.ds(qcols, kvcols)], local_sem.at[1])
+    load = pltpu.make_async_copy(hidden_ref, raw, local_sem.at[2])
+    own_q.start()
+    own_kv.start()
+    load.start()
+
+    barrier = pltpu.get_barrier_semaphore()
+    for other in (sib, xn, yn):
+        pl.semaphore_signal(barrier, inc=1, device_id=(other, z), device_id_type=MESH)
+
+    @pl.when(z > 0)
+    def _():
+        pl.semaphore_signal(barrier, inc=1, device_id=(me, z - 1), device_id_type=MESH)
+
+    @pl.when(z < nz - 1)
+    def _():
+        pl.semaphore_signal(barrier, inc=1, device_id=(me, z + 1), device_id_type=MESH)
+
+    pl.semaphore_wait(barrier, 3 + jnp.minimum(z, 1) + jnp.minimum(nz - 1 - z, 1))
+    own_q.wait()
+    own_kv.wait()
+
+    def copy(way, src, plane, k):
+        piece = wbuf.at[src, plane, pl.ds(pl.multiple_of(k * step, step), step), :]
+        target = {
+            TO_X: (xn, z), TO_Y: (yn, z), TO_SIB: (sib, z),
+            TO_UP: (me, z + 1), TO_DOWN: (me, z - 1),
+        }[way]
+        return pltpu.make_async_remote_copy(
+            src_ref=piece, dst_ref=piece,
+            send_sem=send_sem.at[way, src // 2, plane, k],
+            recv_sem=recv_sem.at[src, plane, k],
+            device_id=target, device_id_type=MESH,
+        )
+
+    def ways(rel, hop, sign):
+        always = lambda k: True
+        first = lambda k: lax.rem(k, 2) == 0
+        second = lambda k: lax.rem(k, 2) == 1
+        is_late = lambda k: k < late
+        not_late = lambda k: k >= late
+        found = []
+        if hop == 0:
+            up = always if rel == OWN else is_late
+            found += [(TO_UP, up, z < nz - 1), (TO_DOWN, up, z > 0)]
+            if rel == OWN:
+                found += [(TO_X, always, True), (TO_Y, always, True)]
+            if rel == VIA_X:
+                found += [(TO_Y, first, True)]
+            if rel == VIA_Y:
+                found += [(TO_X, second, True)]
+        else:
+            onward = (TO_UP, z < nz - 1) if sign > 0 else (TO_DOWN, z > 0)
+            found += [(onward[0], always if rel == OWN else is_late, onward[1])]
+            if rel == OWN:
+                found += [(TO_X, not_late, True), (TO_Y, not_late, True)]
+            if rel == VIA_X:
+                found += [(TO_Y, lambda k: (k >= late) & first(k), True)]
+            if rel == VIA_Y:
+                found += [(TO_X, lambda k: (k >= late) & second(k), True)]
+        return found + [(TO_SIB, always, True)]
+
+    def place(hop, sign):
+        plane = z - sign * hop
+        return plane, (plane >= 0) & (plane < nz)
+
+    def both(a, b):
+        if a is True:
+            return b
+        return a if b is True else a & b
+
+    def guarded(cond, do):
+        if cond is True:
+            do()
+        else:
+            pl.when(cond)(do)
+
+    def arrive(rel, hop, sign, k):
+        plane, _ = place(hop, sign)
+        src = source[rel]
+        if not (rel == OWN and hop == 0):
+            copy(TO_SIB, src, plane, k).wait_recv()
+        for way, cond, reach in ways(rel, hop, sign):
+            guarded(both(cond(k), reach), lambda way=way: copy(way, src, plane, k).start())
+
+    def each(slots):
+        def body(k, carry):
+            for rel, hop, sign in slots:
+                guarded(True if hop == 0 else place(hop, sign)[1],
+                        lambda rel=rel, hop=hop, sign=sign: arrive(rel, hop, sign, k))
+            return carry
+        lax.fori_loop(0, pieces, body, 0)
+
+    def signs(hop):
+        return (1,) if hop == 0 else (1, -1)
+
+    def multiply(hop, lane):
+        for sign in signs(hop):
+            plane, ok = place(hop, sign)
+
+            def body(j, carry):
+                base = lax.rem(me // 2 + j, ndp // 2) * 2
+                src = base + (core if lane == 0 else 1 - core)
+                if lane == 1:
+                    def take(k, c):
+                        copy(TO_SIB, src, plane, k).wait_recv()
+                        return c
+                    lax.fori_loop(0, pieces, take, 0)
+                acc[plane] += jnp.dot(
+                    normed[src], wbuf[src, plane], preferred_element_type=jnp.float32
+                )
+                return carry
+
+            def run():
+                lax.fori_loop(0, ndp // 2, body, 0)
+            guarded(True if hop == 0 else ok, run)
+
+    each([(OWN, 0, 1)])
+
+    load.wait()
+    group = 16
+
+    def norm_rows(i, carry):
+        at = pl.ds(pl.multiple_of(i * group, group), group)
+        value = raw[at, :].astype(jnp.float32)
+        mean = jnp.sum(value * value, axis=-1, keepdims=True) * (1.0 / width)
+        scaled = value * lax.rsqrt(mean + 1e-06) * gain_ref[...].astype(jnp.float32)
+        scaled = scaled.astype(jnp.bfloat16)
+        for d in range(ndp):
+            normed[d, at, :] = scaled[:, d * depth:(d + 1) * depth]
+        return carry
+
+    lax.fori_loop(0, rows // group, norm_rows, 0)
+    for f in range(nz):
+        acc[f, :, 0:qcols] = jnp.broadcast_to(
+            qb_ref[:, f * qcols:(f + 1) * qcols].astype(jnp.float32), (rows, qcols))
+        acc[f, :, qcols:cols] = jnp.broadcast_to(
+            kvb_ref[:, f * kvcols:(f + 1) * kvcols].astype(jnp.float32), (rows, kvcols))
+    each([(VIA_X, 0, 1), (VIA_Y, 0, 1)])
+
+    seg_row = seg_ref[...].astype(jnp.float32)
+    for b in range(rows // BLOCK):
+        at = slice(b * BLOCK, (b + 1) * BLOCK)
+        mine = jnp.transpose(jnp.broadcast_to(seg_row[:, at], (BLOCK, BLOCK)))[:, 0:1]
+        ids = lax.broadcasted_iota(jnp.int32, (BLOCK, rows), 1).astype(jnp.float32)
+        start = jnp.min(jnp.where(mine == seg_row, ids, float(rows)), axis=1, keepdims=True)
+        here = (lax.broadcasted_iota(jnp.int32, (BLOCK, 1), 0) + b * BLOCK).astype(jnp.float32)
+        position = here - start
+        lane = lax.broadcasted_iota(jnp.int32, (BLOCK, HEAD_DIM), 1)
+        half = HEAD_DIM // 2
+        entry = jnp.where(lane < half, lane, lane - half).astype(jnp.float32)
+        frequency = jnp.exp(entry * (-2.0 / HEAD_DIM) * jnp.log(jnp.float32(1000000.0)))
+        angle = position * frequency
+        cos_t[at, :] = jnp.cos(angle)
+        sin_t[at, :] = jnp.where(lane < half, -1.0, 1.0) * jnp.sin(angle)
+
+    for hop in range(nz):
+        after = hop + 1
+        if after < nz:
+            each([(OWN, after, s) for s in signs(after)])
+        if hop > 0:
+            multiply(hop - 1, 1)
+        each([(DIAG, hop, s) for s in signs(hop)])
+        if after < nz:
+            each([(r, after, s) for s in signs(after) for r in (VIA_X, VIA_Y)])
+        multiply(hop, 0)
+    multiply(nz - 1, 1)
+
+    q_heads, kv_heads = qcols // HEAD_DIM, kvcols // HEAD_DIM
+
+    def rotated(value, at):
+        return (value * cos_t[at, :] + pltpu.roll(value, HEAD_DIM // 2, 1) * sin_t[at, :]).astype(jnp.bfloat16)
+
+    def finish(b, carry):
+        at = pl.ds(pl.multiple_of(b * BLOCK, BLOCK), BLOCK)
+        for f in range(nz):
+            for h in range(q_heads):
+                g = f * q_heads + h
+                q_out[at, g * HEAD_DIM:(g + 1) * HEAD_DIM] = rotated(
+                    acc[f, at, h * HEAD_DIM:(h + 1) * HEAD_DIM], at)
+            for h in range(kv_heads):
+                g = f * kv_heads + h
+                value = acc[f, at, qcols + h * HEAD_DIM:qcols + (h + 1) * HEAD_DIM]
+                if g < nz * kv_heads // 2:
+                    k_out[at, g * HEAD_DIM:(g + 1) * HEAD_DIM] = rotated(value, at)
+                else:
+                    g -= nz * kv_heads // 2
+                    v_out[at, g * HEAD_DIM:(g + 1) * HEAD_DIM] = value.astype(jnp.bfloat16)
+        return carry
+
+    lax.fori_loop(0, rows // BLOCK, finish, 0)
+
+    def drain(slots):
+        def body(k, carry):
+            for rel, hop, sign in slots:
+                plane, ok = place(hop, sign)
+
+                def wait_all(rel=rel, hop=hop, sign=sign, plane=plane):
+                    for way, cond, reach in ways(rel, hop, sign):
+                        guarded(both(cond(k), reach),
+                                lambda way=way: copy(way, source[rel], plane, k).wait_send())
+                guarded(True if hop == 0 else ok, wait_all)
+            return carry
+        lax.fori_loop(0, pieces, body, 0)
+
+    for hop in range(nz):
+        for s in signs(hop):
+            drain([(r, hop, s) for r in (OWN, VIA_X, VIA_Y, DIAG)])
+
+
+def gather_project(ndp, nz, hidden, norm_gain, q_weight, kv_weight, q_bias, kv_bias, seg):
+    rows, width = hidden.shape
+    depth, qcols = q_weight.shape
+    kvcols = kv_weight.shape[1]
+    pieces, late = 5, 1
+    vmem = pl.BlockSpec(memory_space=pltpu.VMEM)
+    hbm = pl.BlockSpec(memory_space=pl.ANY)
+    bf16, f32 = jnp.bfloat16, jnp.float32
+    return pl.pallas_call(
+        functools.partial(gather_project_kernel, ndp, nz, pieces, late),
+        out_shape=[
+            jax.ShapeDtypeStruct((rows, qcols * nz), bf16),
+            jax.ShapeDtypeStruct((rows, kvcols * nz // 2), bf16),
+            jax.ShapeDtypeStruct((rows, kvcols * nz // 2), bf16),
+        ],
+        in_specs=[hbm, vmem, hbm, hbm, vmem, vmem, vmem],
+        out_specs=[vmem] * 3,
+        scratch_shapes=[
+            pltpu.VMEM((ndp, nz, depth, qcols + kvcols), bf16),
+            pltpu.VMEM((rows, width), bf16),
+            pltpu.VMEM((ndp, rows, depth), bf16),
+            pltpu.VMEM((nz, rows, qcols + kvcols), f32),
+            pltpu.VMEM((rows, HEAD_DIM), f32),
+            pltpu.VMEM((rows, HEAD_DIM), f32),
+            pltpu.SemaphoreType.DMA((3,)),
+            pltpu.SemaphoreType.DMA((5, ndp // 2, nz, pieces)),
+            pltpu.SemaphoreType.DMA((ndp, nz, pieces)),
+        ],
+        compiler_params=pltpu.CompilerParams(
+            collective_id=0, has_side_effects=True, vmem_limit_bytes=60 * 2**20),
+        cost_estimate=pl.CostEstimate(
+            flops=2 * rows * width * nz * (qcols + kvcols),
+            bytes_accessed=2 * rows * width, transcendentals=0),
+        name="gather_project",
+    )(hidden, norm_gain.reshape(1, -1), q_weight, kv_weight,
+      q_bias.reshape(1, -1), kv_bias.reshape(1, -1), seg)
+
+
+def attend_kernel(q_ref, k_ref, v_ref, seg_ref, out_ref):
+    rows = q_ref.shape[0]
+    group = HEADS // KV_HEADS
+    seg_row = seg_ref[...].astype(jnp.float32)
+    for b in range(rows // BLOCK):
+        at = slice(b * BLOCK, (b + 1) * BLOCK)
+        seen = (b + 1) * BLOCK
+        mine = jnp.transpose(jnp.broadcast_to(seg_row[:, at], (BLOCK, BLOCK)))[:, 0:1]
+        r = lax.broadcasted_iota(jnp.int32, (BLOCK, seen), 0) + b * BLOCK
+        s = lax.broadcasted_iota(jnp.int32, (BLOCK, seen), 1)
+        allowed = (mine == seg_row[:, 0:seen]) & (s <= r) & (mine >= 0)
+        live = mine >= 0
+
+        def head_group(g, carry):
+            kv_at = pl.ds(pl.multiple_of(g * HEAD_DIM, HEAD_DIM), HEAD_DIM)
+            keys = k_ref[0:seen, kv_at]
+            values = v_ref[0:seen, kv_at]
+            for h in range(group):
+                q_at = pl.ds(pl.multiple_of((g * group + h) * HEAD_DIM, HEAD_DIM), HEAD_DIM)
+                scores = lax.dot_general(
+                    q_ref[at, q_at], keys, (((1,), (1,)), ((), ())),
+                    preferred_element_type=jnp.float32) * HEAD_DIM ** (-0.5)
+                scores = jnp.where(allowed, scores, -1e30)
+                e = jnp.exp(scores - jnp.max(scores, axis=-1, keepdims=True))
+                p = (e * (1.0 / jnp.sum(e, axis=-1, keepdims=True))).astype(jnp.bfloat16)
+                c = jnp.dot(p, values, preferred_element_type=jnp.float32)
+                out_ref[at, q_at] = jnp.where(live, c, 0.0).astype(out_ref.dtype)
+            return carry
+
+        lax.fori_loop(0, KV_HEADS, head_group, 0)
+
+
+def attend_rows(queries, key_rows, values, seg):
+    vmem = pl.BlockSpec(memory_space=pltpu.VMEM)
+    return pl.pallas_call(
+        attend_kernel,
+        out_shape=jax.ShapeDtypeStruct(queries.shape, jnp.bfloat16),
+        in_specs=[vmem] * 4,
+        out_specs=vmem,
+        compiler_params=pltpu.CompilerParams(vmem_limit_bytes=32 * 2**20),
+        name="attend_rows",
+    )(queries, key_rows, values, seg)
 
 
 def positions_of(segments):
@@ -107,7 +430,14 @@
     return (queries, key_rows, values)
 
 
-def local(hidden, norm_gain, q_weight, kv_weight, q_bias, kv_bias, segments):
+def local(ndp, nz, hidden, norm_gain, q_weight, kv_weight, q_bias, kv_bias, segments):
+    planes_fit = ndp == 2 * 2 * 2
+    heads_fit = q_weight.shape[1] % HEAD_DIM == 0 and kv_weight.shape[1] % HEAD_DIM == 0
+    if planes_fit and heads_fit:
+        seg = segments.reshape(1, -1)
+        queries, key_rows, values = gather_project(
+            ndp, nz, hidden, norm_gain, q_weight, kv_weight, q_bias, kv_bias, seg)
+        return attend_rows(queries, key_rows, values, seg)
     normed = normalize(hidden, norm_gain)
     positions = positions_of(segments)
     queries, key_rows, values = project(normed, positions, q_weight, kv_weight, q_bias, kv_bias)
@@ -125,4 +455,5 @@
         P(("dp", "fsdp")),
     )
     out_specs = P(("dp", "fsdp"), None)
-    return jax.shard_map(local, mesh=mesh, in_specs=in_specs, out_specs=out_specs, check_vma=False)
+    return jax.shard_map(
+        functools.partial(local, mesh.shape["dp"], mesh.shape["fsdp"]), mesh=mesh, in_specs=in_specs, out_specs=out_specs, check_vma=False)

time: 386 us -> 188 us (0.49)
  waiting for transfers between devices: 283 us -> 0 us
  Pallas kernels: 0 us -> 179 us
  matrix products: 41.3 us -> 0 us
  other arithmetic: 25.3 us -> 0 us
  local copies, waits for them, and re-layouts: 22.7 us -> 8.69 us
  between operations: 13.4 us -> 0.03 us
    all_gather x4 -> x0, waiting for transfers between devices: 281 us -> none  [the longest x1 119 us: project(): q_lin = add_rows(lax.all_gather(q_rows_full, 'dp', axis=0, tiled=True))]
    pallas_call x0 -> x2, Pallas kernels: none -> 179 us  [the longest x1 159 us: gather_project(): pl.pallas_call(functools.partial(gather_project_kernel, ndp, nz, pieces,...]
    dot_general x4 -> x0, matrix products: 41.3 us -> none  [the longest x2 26 us: add_rows(): return jnp.dot(row_input, piece_rows, preferred_element_type=jnp.float32)]
    sub x1 -> x0, other arithmetic: 16.9 us -> none  [attend(): exponents = jnp.exp(scores - row_max)]
    concatenate x8 -> x0, local copies, waits for them, and re-layouts: 7.37 us -> none  [rotate(): jnp.concatenate([lower_half * cosine - second * sine_part, second * cosin...]
    convert_element_type x4 -> x0, local copies, waits for them, and re-layouts: 7.15 us -> none  [the longest x2 6.8 us: attend(): return context.reshape(row_count, HEADS * HEAD_DIM).astype(jnp.bfloat16)]
    add x1 -> x0, local copies, waits for them, and re-layouts: 5.49 us -> none  [project(): q_lin = q_lin + q_bias.astype(jnp.float32)]
    reshape x1 -> x4, local copies, waits for them, and re-layouts: 0.26 us -> 5.15 us  [the longest x1 1.32 us: gather_project(): norm_gain.reshape(1, -1)]
  transfers between devices with their start and end apart: 4 -> 0, of which waited for: 4 -> 0; matrix products, arithmetic and copies ran while one was open for 4% -> 0% of each run, Pallas kernels for 0% -> 0%
where the time goes in v1:
time: 188 us
  Pallas kernels  179 us (95%)
  local copies, waits for them, and re-layouts  8.69 us (5%)
    pallas_call x1, Pallas kernels, gather_project(): pl.pallas_call(functools.partial(gather_project_kernel, ndp, nz, pieces,...  159 us
    pallas_call x1, Pallas kernels, attend_rows(): pl.pallas_call(attend_kernel, out_shape=jax.ShapeDtypeStruct(queries.shap...  19.9 us

profile of v1, /device:TPU:0, one launch (start us, length us, event | category | flops | bytes accessed | tf_op | source)
XLA Modules:
  0.0 187.9 jit_solution(16785916836084058421)
XLA Ops:
  0.0 1.3 reshape.15.seg_ref
  1.3 1.3 reshape.14.kvb_ref
  2.5 1.3 reshape.13.qb_ref
  3.8 1.3 reshape.12.gain_ref
  5.2 0.0 copy-start.3
  5.2 159.3 %gather_project.1 = (bf16[384,2560]{1,0:T(8,128)(2,1)}, bf16[384,512]{1,0:T(8,128)(2,1)}, bf16[384,512]{1,0:T(8,128)(2,1)}) custom-call(bf16[384,5120]{1,0:T(8,128)(2,1)} %hidden_ref.1, bf16[1,5120]{1,0:T(2,128)(2,1)} %reshape.12.gain_ref, bf16[640,640]{1,0:T(8,128)(2,1)} %qw_ref.1, bf16[640,256]{1,0:T(8,128)(2,1)} %kvw_ref.1, ...), custom_call_target="tpu_custom_call" | custom-call | flops 14092861440 | bytes 3932160 | tf_op jit(solution)/shard_map/gather_project/pallas_call | solution.py:261
  164.5 0.0 copy-done.3
  164.5 0.0 copy-start
  164.5 1.5 copy-done
  166.0 0.0 copy-start.1
  166.0 1.0 copy-done.1
  167.0 0.0 copy-start.2
  167.0 1.0 copy-done.2
  168.0 19.9 %attend_rows.1 = bf16[384,2560]{1,0:T(8,128)(2,1)} custom-call(bf16[384,2560]{1,0:T(8,128)(2,1)S(1)} %copy-done, bf16[384,512]{1,0:T(8,128)(2,1)S(1)} %copy-done.1, bf16[384,512]{1,0:T(8,128)(2,1)S(1)} %copy-done.2, s32[1,384]{1,0:T(1,128)S(1)} %copy-done.3), custom_call_target="tpu_custom_call" | custom-call | tf_op jit(solution)/shard_map/attend_rows/pallas_call | solution.py:325
Async XLA Ops:
  5.2 159.3 %copy-start.3 = (s32[1,384]{1,0:T(1,128)S(1)}, s32[1,384]{1,0:T(1,128)}, u32[]{:S(2)}) copy-start(s32[1,384]{1,0:T(1,128)} %reshape.15.seg_ref) | copy-start | bytes 4612
  164.5 1.5 copy-start
  166.0 1.0 copy-start.1
  167.0 1.0 copy-start.2

commit v2 on v0

--- a/solution.py
+++ b/solution.py
@@ -1,12 +1,366 @@
+import functools
+
 import jax
 import jax.numpy as jnp
 from jax import lax
+from jax.experimental import pallas as pl
+from jax.experimental.pallas import tpu as pltpu
 from jax.sharding import PartitionSpec as P
 
 HEADS = 20
 KV_HEADS = 4
 HEAD_DIM = 128
 BLOCK = 128
+LANES = 128
+MESH = pl.DeviceIdType.MESH
+TO_X, TO_Y, TO_UP, TO_DOWN, TO_SIB = range(5)
+OWN, VIA_X, VIA_Y, DIAG = range(4)
+PIECE, LATE = range(2)
+
+
+def gather_project_kernel(
+    ndp, nz, pieces, late,
+    hidden_ref, qw_ref, kvw_ref, small_ref,
+    out_ref,
+    wbuf, raw, normed, acc, cos_t, sin_t, mask_t, k_buf, v_buf, local_sem, send_sem, recv_sem,
+):
+    rows, width = raw.shape
+    depth, qcols = qw_ref.shape
+    kvcols = kvw_ref.shape[1]
+    cols = qcols + kvcols
+    qb_at = width
+    kvb_at = qb_at + nz * qcols
+    seg_at = kvb_at + nz * kvcols
+    step = depth // pieces
+    me = lax.axis_index("dp")
+    z = lax.axis_index("fsdp")
+    core = lax.rem(me, 2)
+    x = lax.rem(me // 2, 2)
+    y = me // 4
+    sib = me + 1 - 2 * core
+    xn = me + 2 - 4 * x
+    yn = me + 4 - 8 * y
+    dg = xn + yn - me
+    source = [me, xn, yn, dg]
+
+    own_q = pltpu.make_async_copy(qw_ref, wbuf.at[me, z, :, pl.ds(0, qcols)], local_sem.at[0])
+    own_kv = pltpu.make_async_copy(kvw_ref, wbuf.at[me, z, :, pl.ds(qcols, kvcols)], local_sem.at[1])
+    load = pltpu.make_async_copy(hidden_ref, raw, local_sem.at[2])
+    own_q.start()
+    own_kv.start()
+    load.start()
+
+    barrier = pltpu.get_barrier_semaphore()
+    for other in (sib, xn, yn):
+        pl.semaphore_signal(barrier, inc=1, device_id=(other, z), device_id_type=MESH)
+
+    @pl.when(z > 0)
+    def _():
+        pl.semaphore_signal(barrier, inc=1, device_id=(me, z - 1), device_id_type=MESH)
+
+    @pl.when(z < nz - 1)
+    def _():
+        pl.semaphore_signal(barrier, inc=1, device_id=(me, z + 1), device_id_type=MESH)
+
+    pl.semaphore_wait(barrier, 3 + jnp.minimum(z, 1) + jnp.minimum(nz - 1 - z, 1))
+    own_q.wait()
+    own_kv.wait()
+
+    def copy(way, src, plane, k):
+        piece = wbuf.at[src, plane, pl.ds(pl.multiple_of(k * step, step), step), :]
+        target = {
+            TO_X: (xn, z), TO_Y: (yn, z), TO_SIB: (sib, z),
+            TO_UP: (me, z + 1), TO_DOWN: (me, z - 1),
+        }[way]
+        return pltpu.make_async_remote_copy(
+            src_ref=piece, dst_ref=piece,
+            send_sem=send_sem.at[way, src // 2, plane, k],
+            recv_sem=recv_sem.at[src, plane, k],
+            device_id=target, device_id_type=MESH,
+        )
+
+    def ways(kind, rel, hop, sign):
+        always = lambda k: True
+        first = lambda k: lax.rem(k, 2) == 0
+        second = lambda k: lax.rem(k, 2) == 1
+        not_late = lambda k: k >= late
+        up, down = (TO_UP, always, z < nz - 1), (TO_DOWN, always, z > 0)
+        onward = up if sign > 0 else down
+        sibling = (TO_SIB, always, True)
+        if kind == LATE:
+            return [up, down] if hop == 0 else [onward, sibling]
+        if rel == OWN and hop == 0:
+            return [up, down, (TO_X, always, True), (TO_Y, always, True), sibling]
+        if rel == OWN:
+            return [onward, (TO_X, not_late, True), (TO_Y, not_late, True), sibling]
+        if rel == VIA_X:
+            return [(TO_Y, first, True), sibling]
+        if rel == VIA_Y:
+            return [(TO_X, second, True), sibling]
+        return [sibling]
+
+    def place(hop, sign):
+        plane = z - sign * hop
+        return plane, (plane >= 0) & (plane < nz)
+
+    def both(a, b):
+        if a is True:
+            return b
+        return a if b is True else a & b
+
+    def guarded(cond, do):
+        if cond is True:
+            do()
+        else:
+            pl.when(cond)(do)
+
+    def span(kind, rel, hop):
+        if kind == LATE:
+            return 0, late
+        return (0 if rel == OWN or hop == 0 else late), pieces
+
+    def signs(hop):
+        return (1,) if hop == 0 else (1, -1)
+
+    def slots(kind, rels, hop):
+        return [(kind, rel, hop, sign) for sign in signs(hop) for rel in rels]
+
+    def arrive(kind, rel, hop, sign, k):
+        plane, _ = place(hop, sign)
+        src = source[rel]
+        if hop > 0 or (rel != OWN and kind == PIECE):
+            copy(TO_SIB, src, plane, k).wait_recv()
+        for way, cond, reach in ways(kind, rel, hop, sign):
+            guarded(both(cond(k), reach), lambda way=way: copy(way, src, plane, k).start())
+
+    def each(todo, extra=None):
+        low = min(span(*slot[:3])[0] for slot in todo)
+        high = max(span(*slot[:3])[1] for slot in todo)
+
+        def body(k, carry):
+            for kind, rel, hop, sign in todo:
+                begin, _ = span(kind, rel, hop)
+                cond = True if hop == 0 else place(hop, sign)[1]
+                if begin > low:
+                    cond = both(k >= begin, cond)
+                guarded(cond, lambda slot=(kind, rel, hop, sign): arrive(*slot, k))
+            if extra is not None:
+                count, work = extra
+                per = -(-count // (high - low))
+
+                def some(i, c):
+                    work(i)
+                    return c
+                lax.fori_loop(jnp.minimum((k - low) * per, count),
+                              jnp.minimum((k - low + 1) * per, count), some, 0)
+            return carry
+        lax.fori_loop(low, high, body, 0)
+
+    def multiply_one(hop, sign, rel, lane):
+        plane, ok = place(hop, sign)
+        base = me + lax.rem(rel, 2) * (xn - me) + (rel // 2) * (yn - me)
+        src = base + lane * (sib - me)
+
+        def run():
+            @pl.when(lane == 1)
+            def _():
+                def take(k, c):
+                    copy(TO_SIB, src, plane, k).wait_recv()
+                    return c
+                lax.fori_loop(0, pieces, take, 0)
+            acc[plane] += jnp.dot(
+                normed[src], wbuf[src, plane], preferred_element_type=jnp.float32
+            )
+        guarded(True if hop == 0 else ok, run)
+
+    def multiply(hop, lane, low=0, high=4):
+        def body(i, carry):
+            sign = 1 if hop == 0 else 1 - 2 * lax.rem(i, 2)
+            rel = low + (i if hop == 0 else i // 2)
+            multiply_one(hop, sign, rel, jnp.int32(lane))
+            return carry
+        lax.fori_loop(0, (high - low) * len(signs(hop)), body, 0)
+
+    each(slots(PIECE, [OWN], 0))
+
+    load.wait()
+    group = 16
+
+    def norm_rows(i, carry):
+        at = pl.ds(pl.multiple_of(i * group, group), group)
+        value = raw[at, :].astype(jnp.float32)
+        mean = jnp.sum(value * value, axis=-1, keepdims=True) * (1.0 / width)
+        scaled = value * lax.rsqrt(mean + 1e-06) * small_ref[:, 0:width]
+        scaled = scaled.astype(jnp.bfloat16)
+        for d in range(ndp):
+            normed[d, at, :] = scaled[:, d * depth:(d + 1) * depth]
+        return carry
+
+    lax.fori_loop(0, rows // group, norm_rows, 0)
+    for f in range(nz):
+        acc[f, :, 0:qcols] = jnp.broadcast_to(
+            small_ref[:, qb_at + f * qcols:qb_at + (f + 1) * qcols], (rows, qcols))
+        acc[f, :, qcols:cols] = jnp.broadcast_to(
+            small_ref[:, kvb_at + f * kvcols:kvb_at + (f + 1) * kvcols], (rows, kvcols))
+    each(slots(PIECE, [VIA_X, VIA_Y], 0) + slots(PIECE, [OWN], 1))
+
+    seg_row = small_ref[:, seg_at:seg_at + rows]
+    for b in range(rows // BLOCK):
+        at = slice(b * BLOCK, (b + 1) * BLOCK)
+        mine = jnp.transpose(jnp.broadcast_to(seg_row[:, at], (BLOCK, BLOCK)))[:, 0:1]
+        ids = lax.broadcasted_iota(jnp.int32, (BLOCK, rows), 1).astype(jnp.float32)
+        start = jnp.min(jnp.where(mine == seg_row, ids, float(rows)), axis=1, keepdims=True)
+        here = (lax.broadcasted_iota(jnp.int32, (BLOCK, 1), 0) + b * BLOCK).astype(jnp.float32)
+        position = here - start
+        lane = lax.broadcasted_iota(jnp.int32, (BLOCK, HEAD_DIM), 1)
+        half = HEAD_DIM // 2
+        entry = jnp.where(lane < half, lane, lane - half).astype(jnp.float32)
+        frequency = jnp.exp(entry * (-2.0 / HEAD_DIM) * jnp.log(jnp.float32(1000000.0)))
+        angle = position * frequency
+        cos_t[at, :] = jnp.cos(angle)
+        sin_t[at, :] = jnp.where(lane < half, -1.0, 1.0) * jnp.sin(angle)
+        allowed = (mine == seg_row) & (ids <= here) & (mine >= 0.0)
+        mask_t[at, 0:rows] = jnp.where(allowed, 1.0, 0.0)
+        mask_t[at, rows:] = jnp.broadcast_to(jnp.where(mine >= 0.0, 1.0, 0.0), (BLOCK, LANES))
+
+    group = HEADS // KV_HEADS
+    key_planes = nz // 2
+    per_plane = kvcols // HEAD_DIM
+
+    def rotated(value, at):
+        return (value * cos_t[at, :] + pltpu.roll(value, HEAD_DIM // 2, 1) * sin_t[at, :]).astype(jnp.bfloat16)
+
+    def prepare(g):
+        at = slice(0, rows)
+        lanes = pl.ds(pl.multiple_of(qcols + lax.rem(g, per_plane) * HEAD_DIM, HEAD_DIM), HEAD_DIM)
+        k_buf[g] = rotated(acc[g // per_plane, :, lanes], at)
+        v_buf[g] = acc[key_planes + g // per_plane, :, lanes].astype(jnp.bfloat16)
+
+    scale = HEAD_DIM ** (-0.5) * 1.4426950408889634
+
+    def attend_head(g, h):
+        lanes = pl.ds(pl.multiple_of(h * HEAD_DIM, HEAD_DIM), HEAD_DIM)
+        out_lanes = pl.ds(pl.multiple_of((g * group + h) * HEAD_DIM, HEAD_DIM), HEAD_DIM)
+        for b in range(rows // BLOCK):
+            at = slice(b * BLOCK, (b + 1) * BLOCK)
+            seen = (b + 1) * BLOCK
+            query = rotated(acc[g, at, lanes], at)
+            scores = lax.dot_general(
+                query, k_buf[g, 0:seen, :], (((1,), (1,)), ((), ())),
+                preferred_element_type=jnp.float32)
+            scores = jnp.where(mask_t[at, 0:seen] > 0.5, scores * scale, -1e30)
+            top = jnp.max(scores, axis=-1, keepdims=True)
+            e = jnp.exp2(scores - top)
+            share = mask_t[at, rows:rows + 1] / jnp.sum(e, axis=-1, keepdims=True)
+            p = (e * share).astype(jnp.bfloat16)
+            c = jnp.dot(p, v_buf[g, 0:seen, :], preferred_element_type=jnp.float32)
+            out_ref[at, out_lanes] = c.astype(out_ref.dtype)
+
+    def heads_of(first):
+        def work(i):
+            attend_head(first + i // group, lax.rem(i, group))
+        return KV_HEADS // 2 * group, work
+
+    near_first = (z // (nz // 2)) * (KV_HEADS // 2)
+    far_first = KV_HEADS // 2 - near_first
+    last = nz - 1
+
+    each(slots(PIECE, [OWN], 2) + slots(PIECE, [DIAG], 0))
+    multiply(0, 0)
+    each(slots(PIECE, [VIA_X, VIA_Y], 1))
+    each(slots(LATE, [VIA_X, VIA_Y, DIAG], 0))
+    multiply(0, 1)
+    each(slots(PIECE, [OWN], 3))
+    each(slots(PIECE, [DIAG], 1))
+    each(slots(LATE, [VIA_X, VIA_Y, DIAG], 1))
+    multiply(1, 0)
+    each(slots(PIECE, [VIA_X, VIA_Y], 2))
+    multiply(1, 1)
+    each(slots(LATE, [VIA_X, VIA_Y, DIAG], 2))
+    each(slots(PIECE, [DIAG], 2))
+    multiply(2, 0)
+    multiply(2, 1)
+    prepare(near_first)
+    prepare(near_first + 1)
+    each(slots(PIECE, [VIA_X, VIA_Y], last), heads_of(near_first))
+    each(slots(LATE, [VIA_X, VIA_Y, DIAG], last))
+
+    last_sign = 1 - 2 * jnp.int32(z < nz // 2)
+
+    def far_shard(i):
+        multiply_one(last, last_sign, lax.rem(i, 3), i // 3)
+
+    each(slots(PIECE, [DIAG], last), (6, far_shard))
+    multiply_one(last, last_sign, jnp.int32(DIAG), jnp.int32(0))
+    multiply_one(last, last_sign, jnp.int32(DIAG), jnp.int32(1))
+    prepare(far_first)
+    prepare(far_first + 1)
+    count, work = heads_of(far_first)
+
+    def rest(i, carry):
+        work(i)
+        return carry
+    lax.fori_loop(0, count, rest, 0)
+
+    def drain(todo):
+        def body(k, carry):
+            for kind, rel, hop, sign in todo:
+                plane, ok = place(hop, sign)
+                begin, end = span(kind, rel, hop)
+                cond = True if hop == 0 else ok
+                if begin > 0:
+                    cond = both(k >= begin, cond)
+                if end < pieces:
+                    cond = both(k < end, cond)
+
+                def wait_all(kind=kind, rel=rel, hop=hop, sign=sign, plane=plane):
+                    for way, sent, reach in ways(kind, rel, hop, sign):
+                        guarded(both(sent(k), reach),
+                                lambda way=way: copy(way, source[rel], plane, k).wait_send())
+                guarded(cond, wait_all)
+            return carry
+        lax.fori_loop(0, pieces, body, 0)
+
+    for hop in range(nz):
+        drain(slots(PIECE, [OWN, VIA_X, VIA_Y, DIAG], hop) + slots(LATE, [VIA_X, VIA_Y, DIAG], hop))
+
+
+def gather_project(ndp, nz, hidden, norm_gain, q_weight, kv_weight, q_bias, kv_bias, segments):
+    rows, width = hidden.shape
+    depth, qcols = q_weight.shape
+    kvcols = kv_weight.shape[1]
+    pieces, late = 10, 2
+    vmem = pl.BlockSpec(memory_space=pltpu.VMEM)
+    hbm = pl.BlockSpec(memory_space=pl.ANY)
+    bf16, f32 = jnp.bfloat16, jnp.float32
+    small = jnp.concatenate(
+        [part.astype(f32) for part in (norm_gain, q_bias, kv_bias, segments)]).reshape(1, -1)
+    return pl.pallas_call(
+        functools.partial(gather_project_kernel, ndp, nz, pieces, late),
+        out_shape=jax.ShapeDtypeStruct((rows, qcols * nz), bf16),
+        in_specs=[hbm, hbm, hbm, vmem],
+        out_specs=vmem,
+        scratch_shapes=[
+            pltpu.VMEM((ndp, nz, depth, qcols + kvcols), bf16),
+            pltpu.VMEM((rows, width), bf16),
+            pltpu.VMEM((ndp, rows, depth), bf16),
+            pltpu.VMEM((nz, rows, qcols + kvcols), f32),
+            pltpu.VMEM((rows, HEAD_DIM), f32),
+            pltpu.VMEM((rows, HEAD_DIM), f32),
+            pltpu.VMEM((rows, rows + LANES), f32),
+            pltpu.VMEM((KV_HEADS, rows, HEAD_DIM), bf16),
+            pltpu.VMEM((KV_HEADS, rows, HEAD_DIM), bf16),
+            pltpu.SemaphoreType.DMA((3,)),
+            pltpu.SemaphoreType.DMA((5, ndp // 2, nz, pieces)),
+            pltpu.SemaphoreType.DMA((ndp, nz, pieces)),
+        ],
+        compiler_params=pltpu.CompilerParams(
+            collective_id=0, has_side_effects=True, vmem_limit_bytes=60 * 2**20),
+        cost_estimate=pl.CostEstimate(
+            flops=2 * rows * width * nz * (qcols + kvcols),
+            bytes_accessed=2 * rows * width, transcendentals=0),
+        name="gather_project_attend",
+    )(hidden, q_weight, kv_weight, small)
 
 
 def positions_of(segments):
@@ -107,7 +461,16 @@
     return (queries, key_rows, values)
 
 
-def local(hidden, norm_gain, q_weight, kv_weight, q_bias, kv_bias, segments):
+def local(ndp, nz, hidden, norm_gain, q_weight, kv_weight, q_bias, kv_bias, segments):
+    planes_fit = ndp == 2 * 2 * 2
+    heads_fit = (
+        nz == KV_HEADS
+        and q_weight.shape[1] == HEADS // KV_HEADS * HEAD_DIM
+        and kv_weight.shape[1] == 2 * HEAD_DIM
+    )
+    if planes_fit and heads_fit:
+        return gather_project(
+            ndp, nz, hidden, norm_gain, q_weight, kv_weight, q_bias, kv_bias, segments)
     normed = normalize(hidden, norm_gain)
     positions = positions_of(segments)
     queries, key_rows, values = project(normed, positions, q_weight, kv_weight, q_bias, kv_bias)
@@ -125,4 +488,5 @@
         P(("dp", "fsdp")),
     )
     out_specs = P(("dp", "fsdp"), None)
-    return jax.shard_map(local, mesh=mesh, in_specs=in_specs, out_specs=out_specs, check_vma=False)
+    return jax.shard_map(
+        functools.partial(local, mesh.shape["dp"], mesh.shape["fsdp"]), mesh=mesh, in_specs=in_specs, out_specs=out_specs, check_vma=False)

time: 386 us -> 202 us (0.52)
  waiting for transfers between devices: 283 us -> 0 us
  Pallas kernels: 0 us -> 195 us
  matrix products: 41.3 us -> 0 us
  other arithmetic: 25.3 us -> 2.77 us
  local copies, waits for them, and re-layouts: 22.7 us -> 3.59 us
  between operations: 13.4 us -> 0.01 us
    all_gather x4 -> x0, waiting for transfers between devices: 281 us -> none  [the longest x1 119 us: project(): q_lin = add_rows(lax.all_gather(q_rows_full, 'dp', axis=0, tiled=True))]
    pallas_call x0 -> x1, Pallas kernels: none -> 195 us  [gather_project(): pl.pallas_call(functools.partial(gather_project_kernel, ndp, nz, pieces,...]
    dot_general x4 -> x0, matrix products: 41.3 us -> none  [the longest x2 26 us: add_rows(): return jnp.dot(row_input, piece_rows, preferred_element_type=jnp.float32)]
    sub x1 -> x0, other arithmetic: 16.9 us -> none  [attend(): exponents = jnp.exp(scores - row_max)]
    concatenate x8 -> x0, local copies, waits for them, and re-layouts: 7.37 us -> none  [rotate(): jnp.concatenate([lower_half * cosine - second * sine_part, second * cosin...]
    convert_element_type x4 -> x0, local copies, waits for them, and re-layouts: 7.15 us -> none  [the longest x2 6.8 us: attend(): return context.reshape(row_count, HEADS * HEAD_DIM).astype(jnp.bfloat16)]
    add x1 -> x0, local copies, waits for them, and re-layouts: 5.49 us -> none  [project(): q_lin = q_lin + q_bias.astype(jnp.float32)]
    another operation x4 -> x0, other arithmetic: 4.13 us -> none
  transfers between devices with their start and end apart: 4 -> 0, of which waited for: 4 -> 0; matrix products, arithmetic and copies ran while one was open for 4% -> 0% of each run, Pallas kernels for 0% -> 0%
where the time goes in v2:
time: 202 us
  Pallas kernels  195 us (97%)
  local copies, waits for them, and re-layouts  3.59 us (2%)
  other arithmetic  2.77 us (1%)
    pallas_call x1, Pallas kernels, gather_project(): pl.pallas_call(functools.partial(gather_project_kernel, ndp, nz, pieces,...  195 us

profile of v2, /device:TPU:0, one launch (start us, length us, event | category | flops | bytes accessed | tf_op | source)
XLA Modules:
  0.0 201.6 jit_solution(15785038150467252012)
XLA Ops:
  0.0 0.7 convert_element_type.15
  0.7 0.7 convert_element_type.14
  1.4 0.7 convert_element_type.13
  2.1 0.7 convert_element_type.12
  2.8 0.6 reshape.3.small_ref
  3.4 195.2 %gather_project_attend.1 = bf16[384,2560]{1,0:T(8,128)(2,1)} custom-call(bf16[384,5120]{1,0:T(8,128)(2,1)} %hidden_ref.1, bf16[640,640]{1,0:T(8,128)(2,1)} %qw_ref.1, bf16[640,256]{1,0:T(8,128)(2,1)} %kvw_ref.1, f32[1,9088]{1,0:T(1,128)} %reshape.3.small_ref), custom_call_target="tpu_custom_call" | custom-call | flops 14092861440 | bytes 3932160 | tf_op jit(solution)/shard_map/gather_project_attend/pallas_call | solution.py:338
  198.7 2.9 %copy.9 = bf16[384,2560]{1,0:T(8,128)(2,1)} copy(bf16[384,2560]{1,0:T(8,128)(2,1)} %gather_project_attend.1) | data formatting | bytes 3932160
  (1 shorter events, 0.0 us)

commit v3 on v2

--- a/solution.py
+++ b/solution.py
@@ -13,7 +13,7 @@
 BLOCK = 128
 LANES = 128
 MESH = pl.DeviceIdType.MESH
-TO_X, TO_Y, TO_UP, TO_DOWN, TO_SIB = range(5)
+TO_X, TO_Y, TO_UP, TO_DOWN = range(4)
 OWN, VIA_X, VIA_Y, DIAG = range(4)
 PIECE, LATE = range(2)
 
@@ -22,7 +22,7 @@
     ndp, nz, pieces, late,
     hidden_ref, qw_ref, kvw_ref, small_ref,
     out_ref,
-    wbuf, raw, normed, acc, cos_t, sin_t, mask_t, k_buf, v_buf, local_sem, send_sem, recv_sem,
+    wbuf, raw, normed, acc, cos_t, sin_t, mask_t, k_buf, v_buf, local_sem, send_sem, share_sem, recv_sem,
 ):
     rows, width = raw.shape
     depth, qcols = qw_ref.shape
@@ -69,14 +69,21 @@
     def copy(way, src, plane, k):
         piece = wbuf.at[src, plane, pl.ds(pl.multiple_of(k * step, step), step), :]
         target = {
-            TO_X: (xn, z), TO_Y: (yn, z), TO_SIB: (sib, z),
-            TO_UP: (me, z + 1), TO_DOWN: (me, z - 1),
+            TO_X: (xn, z), TO_Y: (yn, z), TO_UP: (me, z + 1), TO_DOWN: (me, z - 1),
         }[way]
         return pltpu.make_async_remote_copy(
             src_ref=piece, dst_ref=piece,
-            send_sem=send_sem.at[way, src // 2, plane, k],
+            send_sem=send_sem.at[way, plane],
             recv_sem=recv_sem.at[src, plane, k],
             device_id=target, device_id_type=MESH,
+        )
+
+    def shared(src, plane):
+        shard = wbuf.at[src, plane]
+        return pltpu.make_async_remote_copy(
+            src_ref=shard, dst_ref=shard,
+            send_sem=share_sem, recv_sem=recv_sem.at[src, plane, 0],
+            device_id=(sib, z), device_id_type=MESH,
         )
 
     def ways(kind, rel, hop, sign):
@@ -86,18 +93,17 @@
         not_late = lambda k: k >= late
         up, down = (TO_UP, always, z < nz - 1), (TO_DOWN, always, z > 0)
         onward = up if sign > 0 else down
-        sibling = (TO_SIB, always, True)
         if kind == LATE:
-            return [up, down] if hop == 0 else [onward, sibling]
+            return [up, down] if hop == 0 else [onward]
         if rel == OWN and hop == 0:
-            return [up, down, (TO_X, always, True), (TO_Y, always, True), sibling]
+            return [up, down, (TO_X, always, True), (TO_Y, always, True)]
         if rel == OWN:
-            return [onward, (TO_X, not_late, True), (TO_Y, not_late, True), sibling]
+            return [onward, (TO_X, not_late, True), (TO_Y, not_late, True)]
         if rel == VIA_X:
-            return [(TO_Y, first, True), sibling]
+            return [(TO_Y, first, True)]
         if rel == VIA_Y:
-            return [(TO_X, second, True), sibling]
-        return [sibling]
+            return [(TO_X, second, True)]
+        return []
 
     def place(hop, sign):
         plane = z - sign * hop
@@ -129,7 +135,7 @@
         plane, _ = place(hop, sign)
         src = source[rel]
         if hop > 0 or (rel != OWN and kind == PIECE):
-            copy(TO_SIB, src, plane, k).wait_recv()
+            copy(TO_X, src, plane, k).wait_recv()
         for way, cond, reach in ways(kind, rel, hop, sign):
             guarded(both(cond(k), reach), lambda way=way: copy(way, src, plane, k).start())
 
@@ -156,6 +162,15 @@
             return carry
         lax.fori_loop(low, high, body, 0)
 
+    def share(rels, hop):
+        for sign in signs(hop):
+            plane, ok = place(hop, sign)
+
+            def send(plane=plane):
+                for rel in rels:
+                    shared(source[rel], plane).start()
+            guarded(True if hop == 0 else ok, send)
+
     def multiply_one(hop, sign, rel, lane):
         plane, ok = place(hop, sign)
         base = me + lax.rem(rel, 2) * (xn - me) + (rel // 2) * (yn - me)
@@ -164,10 +179,7 @@
         def run():
             @pl.when(lane == 1)
             def _():
-                def take(k, c):
-                    copy(TO_SIB, src, plane, k).wait_recv()
-                    return c
-                lax.fori_loop(0, pieces, take, 0)
+                shared(src, plane).wait_recv()
             acc[plane] += jnp.dot(
                 normed[src], wbuf[src, plane], preferred_element_type=jnp.float32
             )
@@ -182,6 +194,7 @@
         lax.fori_loop(0, (high - low) * len(signs(hop)), body, 0)
 
     each(slots(PIECE, [OWN], 0))
+    share([OWN], 0)
 
     load.wait()
     group = 16
@@ -203,6 +216,8 @@
         acc[f, :, qcols:cols] = jnp.broadcast_to(
             small_ref[:, kvb_at + f * kvcols:kvb_at + (f + 1) * kvcols], (rows, kvcols))
     each(slots(PIECE, [VIA_X, VIA_Y], 0) + slots(PIECE, [OWN], 1))
+    share([VIA_X, VIA_Y], 0)
+    share([OWN], 1)
 
     seg_row = small_ref[:, seg_at:seg_at + rows]
     for b in range(rows // BLOCK):
@@ -266,24 +281,30 @@
     last = nz - 1
 
     each(slots(PIECE, [OWN], 2) + slots(PIECE, [DIAG], 0))
+    share([DIAG], 0)
+    share([OWN], 2)
     multiply(0, 0)
     each(slots(PIECE, [VIA_X, VIA_Y], 1))
     each(slots(LATE, [VIA_X, VIA_Y, DIAG], 0))
     multiply(0, 1)
     each(slots(PIECE, [OWN], 3))
+    share([OWN], 3)
     each(slots(PIECE, [DIAG], 1))
     each(slots(LATE, [VIA_X, VIA_Y, DIAG], 1))
+    share([VIA_X, VIA_Y, DIAG], 1)
     multiply(1, 0)
     each(slots(PIECE, [VIA_X, VIA_Y], 2))
     multiply(1, 1)
     each(slots(LATE, [VIA_X, VIA_Y, DIAG], 2))
     each(slots(PIECE, [DIAG], 2))
+    share([VIA_X, VIA_Y, DIAG], 2)
     multiply(2, 0)
     multiply(2, 1)
     prepare(near_first)
     prepare(near_first + 1)
     each(slots(PIECE, [VIA_X, VIA_Y], last), heads_of(near_first))
     each(slots(LATE, [VIA_X, VIA_Y, DIAG], last))
+    share([VIA_X, VIA_Y], last)
 
     last_sign = 1 - 2 * jnp.int32(z < nz // 2)
 
@@ -291,6 +312,7 @@
         multiply_one(last, last_sign, lax.rem(i, 3), i // 3)
 
     each(slots(PIECE, [DIAG], last), (6, far_shard))
+    share([DIAG], last)
     multiply_one(last, last_sign, jnp.int32(DIAG), jnp.int32(0))
     multiply_one(last, last_sign, jnp.int32(DIAG), jnp.int32(1))
     prepare(far_first)
@@ -302,34 +324,41 @@
         return carry
     lax.fori_loop(0, count, rest, 0)
 
-    def drain(todo):
-        def body(k, carry):
-            for kind, rel, hop, sign in todo:
-                plane, ok = place(hop, sign)
-                begin, end = span(kind, rel, hop)
-                cond = True if hop == 0 else ok
-                if begin > 0:
-                    cond = both(k >= begin, cond)
-                if end < pieces:
-                    cond = both(k < end, cond)
-
-                def wait_all(kind=kind, rel=rel, hop=hop, sign=sign, plane=plane):
-                    for way, sent, reach in ways(kind, rel, hop, sign):
-                        guarded(both(sent(k), reach),
-                                lambda way=way: copy(way, source[rel], plane, k).wait_send())
-                guarded(cond, wait_all)
-            return carry
-        lax.fori_loop(0, pieces, body, 0)
-
-    for hop in range(nz):
-        drain(slots(PIECE, [OWN, VIA_X, VIA_Y, DIAG], hop) + slots(LATE, [VIA_X, VIA_Y, DIAG], hop))
+    def sent(way, plane, count):
+        some = wbuf.at[pl.ds(0, count), 0, pl.ds(0, step), :]
+        pltpu.make_async_copy(some, some, send_sem.at[way, plane]).wait()
+
+    def flat(plane, carry):
+        @pl.when(plane == z)
+        def _():
+            sent(TO_X, plane, pieces + pieces // 2)
+            sent(TO_Y, plane, pieces + (pieces + 1) // 2)
+
+        @pl.when(plane != z)
+        def _():
+            odd = pieces // 2 - late // 2
+            sent(TO_X, plane, pieces - late + odd)
+            sent(TO_Y, plane, pieces - late + (pieces - late - odd))
+
+        @pl.when((plane <= z) & (z < nz - 1))
+        def _():
+            sent(TO_UP, plane, pieces + 3 * late)
+
+        @pl.when((plane >= z) & (z > 0))
+        def _():
+            sent(TO_DOWN, plane, pieces + 3 * late)
+        return carry
+
+    lax.fori_loop(0, nz, flat, 0)
+    lane_shards = wbuf.at[pl.ds(0, ndp // 2)]
+    pltpu.make_async_copy(lane_shards, lane_shards, share_sem).wait()
 
 
 def gather_project(ndp, nz, hidden, norm_gain, q_weight, kv_weight, q_bias, kv_bias, segments):
     rows, width = hidden.shape
     depth, qcols = q_weight.shape
     kvcols = kv_weight.shape[1]
-    pieces, late = 10, 2
+    pieces, late = 5, 1
     vmem = pl.BlockSpec(memory_space=pltpu.VMEM)
     hbm = pl.BlockSpec(memory_space=pl.ANY)
     bf16, f32 = jnp.bfloat16, jnp.float32
@@ -351,7 +380,8 @@
             pltpu.VMEM((KV_HEADS, rows, HEAD_DIM), bf16),
             pltpu.VMEM((KV_HEADS, rows, HEAD_DIM), bf16),
             pltpu.SemaphoreType.DMA((3,)),
-            pltpu.SemaphoreType.DMA((5, ndp // 2, nz, pieces)),
+            pltpu.SemaphoreType.DMA((4, nz)),
+            pltpu.SemaphoreType.DMA(()),
             pltpu.SemaphoreType.DMA((ndp, nz, pieces)),
         ],
         compiler_params=pltpu.CompilerParams(

time: 202 us -> 195 us (0.965)
  Pallas kernels: 195 us -> 188 us
    pallas_call x1, Pallas kernels: 195 us -> 188 us  [gather_project(): pl.pallas_call(functools.partial(gather_project_kernel, ndp, nz, pieces,...]
where the time goes in v3:
time: 195 us; the launch traced here: 194 us
  Pallas kernels  188 us (96%)
  local copies, waits for them, and re-layouts  3.59 us (2%)
  other arithmetic  2.77 us (1%)
    pallas_call x1, Pallas kernels, gather_project(): pl.pallas_call(functools.partial(gather_project_kernel, ndp, nz, pieces,...  188 us

profile of v3, /device:TPU:0, one launch (start us, length us, event | category | flops | bytes accessed | tf_op | source)
XLA Modules:
  0.0 194.4 jit_solution(14729386514871401137)
XLA Ops:
  0.0 0.7 convert_element_type.15
  0.7 0.7 convert_element_type.14
  1.4 0.7 convert_element_type.13
  2.1 0.7 convert_element_type.12
  2.8 0.6 reshape.3.small_ref
  3.4 188.0 %gather_project_attend.1 = bf16[384,2560]{1,0:T(8,128)(2,1)} custom-call(bf16[384,5120]{1,0:T(8,128)(2,1)} %hidden_ref.1, bf16[640,640]{1,0:T(8,128)(2,1)} %qw_ref.1, bf16[640,256]{1,0:T(8,128)(2,1)} %kvw_ref.1, f32[1,9088]{1,0:T(1,128)} %reshape.3.small_ref), custom_call_target="tpu_custom_call" | custom-call | flops 14092861440 | bytes 3932160 | tf_op jit(solution)/shard_map/gather_project_attend/pallas_call | solution.py:367
  191.5 2.9 %copy.9 = bf16[384,2560]{1,0:T(8,128)(2,1)} copy(bf16[384,2560]{1,0:T(8,128)(2,1)} %gather_project_attend.1) | data formatting | bytes 3932160
  (1 shorter events, 0.0 us)

commit v4 on v3

--- a/solution.py
+++ b/solution.py
@@ -139,7 +139,7 @@
         for way, cond, reach in ways(kind, rel, hop, sign):
             guarded(both(cond(k), reach), lambda way=way: copy(way, src, plane, k).start())
 
-    def each(todo, extra=None):
+    def each(todo, *extra):
         low = min(span(*slot[:3])[0] for slot in todo)
         high = max(span(*slot[:3])[1] for slot in todo)
 
@@ -150,11 +150,10 @@
                 if begin > low:
                     cond = both(k >= begin, cond)
                 guarded(cond, lambda slot=(kind, rel, hop, sign): arrive(*slot, k))
-            if extra is not None:
-                count, work = extra
+            for count, work in extra:
                 per = -(-count // (high - low))
 
-                def some(i, c):
+                def some(i, c, work=work):
                     work(i)
                     return c
                 lax.fori_loop(jnp.minimum((k - low) * per, count),
@@ -185,13 +184,19 @@
             )
         guarded(True if hop == 0 else ok, run)
 
-    def multiply(hop, lane, low=0, high=4):
+    def shards(hop, low, high):
+        ways_in, rels = len(signs(hop)), high - low
+
+        def work(i):
+            j = i // ways_in
+            multiply_one(hop, 1 - 2 * lax.rem(i, ways_in), low + lax.rem(j, rels), j // rels)
+        return ways_in * rels * 2, work
+
+    def run_all(count, work):
         def body(i, carry):
-            sign = 1 if hop == 0 else 1 - 2 * lax.rem(i, 2)
-            rel = low + (i if hop == 0 else i // 2)
-            multiply_one(hop, sign, rel, jnp.int32(lane))
+            work(i)
             return carry
-        lax.fori_loop(0, (high - low) * len(signs(hop)), body, 0)
+        lax.fori_loop(0, count, body, 0)
 
     each(slots(PIECE, [OWN], 0))
     share([OWN], 0)
@@ -253,76 +258,59 @@
 
     scale = HEAD_DIM ** (-0.5) * 1.4426950408889634
 
-    def attend_head(g, h):
-        lanes = pl.ds(pl.multiple_of(h * HEAD_DIM, HEAD_DIM), HEAD_DIM)
-        out_lanes = pl.ds(pl.multiple_of((g * group + h) * HEAD_DIM, HEAD_DIM), HEAD_DIM)
-        for b in range(rows // BLOCK):
+    def attend_group(g):
+        prepare(g)
+        blocks = range(rows // BLOCK)
+        scores, shares = [], []
+        for b in blocks:
             at = slice(b * BLOCK, (b + 1) * BLOCK)
             seen = (b + 1) * BLOCK
-            query = rotated(acc[g, at, lanes], at)
-            scores = lax.dot_general(
+            query = jnp.concatenate([
+                rotated(acc[g, at, h * HEAD_DIM:(h + 1) * HEAD_DIM], at) for h in range(group)], axis=0)
+            score = lax.dot_general(
                 query, k_buf[g, 0:seen, :], (((1,), (1,)), ((), ())),
-                preferred_element_type=jnp.float32)
-            scores = jnp.where(mask_t[at, 0:seen] > 0.5, scores * scale, -1e30)
-            top = jnp.max(scores, axis=-1, keepdims=True)
-            e = jnp.exp2(scores - top)
-            share = mask_t[at, rows:rows + 1] / jnp.sum(e, axis=-1, keepdims=True)
-            p = (e * share).astype(jnp.bfloat16)
+                preferred_element_type=jnp.float32).reshape(group, BLOCK, seen)
+            scores.append(jnp.where(mask_t[at, 0:seen][None] > 0.5, score * scale, -1e30))
+        tops = [jnp.max(score, axis=-1, keepdims=True) for score in scores]
+        scores = [jnp.exp2(score - top) for score, top in zip(scores, tops)]
+        sums = [jnp.sum(score, axis=-1, keepdims=True) for score in scores]
+        for b in blocks:
+            at = slice(b * BLOCK, (b + 1) * BLOCK)
+            seen = (b + 1) * BLOCK
+            share_of = mask_t[at, rows:rows + 1][None] / sums[b]
+            p = (scores[b] * share_of).astype(jnp.bfloat16).reshape(group * BLOCK, seen)
             c = jnp.dot(p, v_buf[g, 0:seen, :], preferred_element_type=jnp.float32)
-            out_ref[at, out_lanes] = c.astype(out_ref.dtype)
-
-    def heads_of(first):
-        def work(i):
-            attend_head(first + i // group, lax.rem(i, group))
-        return KV_HEADS // 2 * group, work
-
-    near_first = (z // (nz // 2)) * (KV_HEADS // 2)
-    far_first = KV_HEADS // 2 - near_first
-    last = nz - 1
-
-    each(slots(PIECE, [OWN], 2) + slots(PIECE, [DIAG], 0))
+            for h in range(group):
+                lanes = pl.ds(pl.multiple_of((g * group + h) * HEAD_DIM, HEAD_DIM), HEAD_DIM)
+                out_ref[at, lanes] = c[h * BLOCK:(h + 1) * BLOCK].astype(out_ref.dtype)
+
+    half_heads = KV_HEADS // 2
+    near_first = (z // (nz // 2)) * half_heads
+    far_first = half_heads - near_first
+
+    each(slots(PIECE, [OWN], 2) + slots(PIECE, [DIAG], 0), shards(0, OWN, DIAG))
     share([DIAG], 0)
     share([OWN], 2)
-    multiply(0, 0)
-    each(slots(PIECE, [VIA_X, VIA_Y], 1))
+    each(slots(PIECE, [VIA_X, VIA_Y], 1), shards(0, DIAG, DIAG + 1), shards(1, OWN, VIA_X))
     each(slots(LATE, [VIA_X, VIA_Y, DIAG], 0))
-    multiply(0, 1)
-    each(slots(PIECE, [OWN], 3))
+    each(slots(PIECE, [OWN], 3), shards(2, OWN, VIA_X))
     share([OWN], 3)
+    each(slots(PIECE, [VIA_X, VIA_Y], 2), shards(3, OWN, VIA_X))
+    each(slots(LATE, [VIA_X, VIA_Y, DIAG], 1))
     each(slots(PIECE, [DIAG], 1))
-    each(slots(LATE, [VIA_X, VIA_Y, DIAG], 1))
     share([VIA_X, VIA_Y, DIAG], 1)
-    multiply(1, 0)
-    each(slots(PIECE, [VIA_X, VIA_Y], 2))
-    multiply(1, 1)
     each(slots(LATE, [VIA_X, VIA_Y, DIAG], 2))
+    each(slots(PIECE, [VIA_X, VIA_Y], 3), shards(1, VIA_X, DIAG + 1))
     each(slots(PIECE, [DIAG], 2))
     share([VIA_X, VIA_Y, DIAG], 2)
-    multiply(2, 0)
-    multiply(2, 1)
-    prepare(near_first)
-    prepare(near_first + 1)
-    each(slots(PIECE, [VIA_X, VIA_Y], last), heads_of(near_first))
-    each(slots(LATE, [VIA_X, VIA_Y, DIAG], last))
-    share([VIA_X, VIA_Y], last)
-
-    last_sign = 1 - 2 * jnp.int32(z < nz // 2)
-
-    def far_shard(i):
-        multiply_one(last, last_sign, lax.rem(i, 3), i // 3)
-
-    each(slots(PIECE, [DIAG], last), (6, far_shard))
-    share([DIAG], last)
-    multiply_one(last, last_sign, jnp.int32(DIAG), jnp.int32(0))
-    multiply_one(last, last_sign, jnp.int32(DIAG), jnp.int32(1))
-    prepare(far_first)
-    prepare(far_first + 1)
-    count, work = heads_of(far_first)
-
-    def rest(i, carry):
-        work(i)
-        return carry
-    lax.fori_loop(0, count, rest, 0)
+    each(slots(LATE, [VIA_X, VIA_Y, DIAG], 3))
+    share([VIA_X, VIA_Y], 3)
+    run_all(*shards(2, VIA_X, DIAG + 1))
+    run_all(half_heads, lambda i: attend_group(near_first + i))
+    each(slots(PIECE, [DIAG], 3), shards(3, VIA_X, DIAG))
+    share([DIAG], 3)
+    run_all(*shards(3, DIAG, DIAG + 1))
+    run_all(half_heads, lambda i: attend_group(far_first + i))
 
     def sent(way, plane, count):
         some = wbuf.at[pl.ds(0, count), 0, pl.ds(0, step), :]

time: 195 us -> 167 us (0.86)
  Pallas kernels: 188 us -> 159 us
    pallas_call x1, Pallas kernels: 188 us -> 159 us  [gather_project(): pl.pallas_call(functools.partial(gather_project_kernel, ndp, nz, pieces,...]
where the time goes in v4:
time: 167 us; the launch traced here: 165 us
  Pallas kernels  159 us (95%)
  local copies, waits for them, and re-layouts  3.59 us (2%)
  other arithmetic  2.77 us (2%)
    pallas_call x1, Pallas kernels, gather_project(): pl.pallas_call(functools.partial(gather_project_kernel, ndp, nz, pieces,...  159 us

profile of v4, /device:TPU:0, one launch (start us, length us, event | category | flops | bytes accessed | tf_op | source)
XLA Modules:
  0.0 165.0 jit_solution(9583416985673947722)
XLA Ops:
  0.0 0.7 convert_element_type.15
  0.7 0.7 convert_element_type.14
  1.4 0.7 convert_element_type.13
  2.1 0.7 convert_element_type.12
  2.8 0.6 reshape.3.small_ref
  3.4 158.6 %gather_project_attend.1 = bf16[384,2560]{1,0:T(8,128)(2,1)} custom-call(bf16[384,5120]{1,0:T(8,128)(2,1)} %hidden_ref.1, bf16[640,640]{1,0:T(8,128)(2,1)} %qw_ref.1, bf16[640,256]{1,0:T(8,128)(2,1)} %kvw_ref.1, f32[1,9088]{1,0:T(1,128)} %reshape.3.small_ref), custom_call_target="tpu_custom_call" | custom-call | flops 14092861440 | bytes 3932160 | tf_op jit(solution)/shard_map/gather_project_attend/pallas_call | solution.py:355
  162.0 2.9 %copy.9 = bf16[384,2560]{1,0:T(8,128)(2,1)} copy(bf16[384,2560]{1,0:T(8,128)(2,1)} %gather_project_attend.1) | data formatting | bytes 3932160
  (1 shorter events, 0.0 us)

commit v5 on v4

--- a/solution.py
+++ b/solution.py
@@ -20,7 +20,7 @@
 
 def gather_project_kernel(
     ndp, nz, pieces, late,
-    hidden_ref, qw_ref, kvw_ref, small_ref,
+    hidden_ref, qw_ref, kvw_ref, gain_ref, qb_ref, kvb_ref, seg_ref,
     out_ref,
     wbuf, raw, normed, acc, cos_t, sin_t, mask_t, k_buf, v_buf, local_sem, send_sem, share_sem, recv_sem,
 ):
@@ -28,9 +28,6 @@
     depth, qcols = qw_ref.shape
     kvcols = kvw_ref.shape[1]
     cols = qcols + kvcols
-    qb_at = width
-    kvb_at = qb_at + nz * qcols
-    seg_at = kvb_at + nz * kvcols
     step = depth // pieces
     me = lax.axis_index("dp")
     z = lax.axis_index("fsdp")
@@ -204,11 +201,13 @@
     load.wait()
     group = 16
 
+    gain = gain_ref[...].astype(jnp.float32).reshape(1, -1)
+
     def norm_rows(i, carry):
         at = pl.ds(pl.multiple_of(i * group, group), group)
         value = raw[at, :].astype(jnp.float32)
         mean = jnp.sum(value * value, axis=-1, keepdims=True) * (1.0 / width)
-        scaled = value * lax.rsqrt(mean + 1e-06) * small_ref[:, 0:width]
+        scaled = value * lax.rsqrt(mean + 1e-06) * gain
         scaled = scaled.astype(jnp.bfloat16)
         for d in range(ndp):
             normed[d, at, :] = scaled[:, d * depth:(d + 1) * depth]
@@ -217,14 +216,14 @@
     lax.fori_loop(0, rows // group, norm_rows, 0)
     for f in range(nz):
         acc[f, :, 0:qcols] = jnp.broadcast_to(
-            small_ref[:, qb_at + f * qcols:qb_at + (f + 1) * qcols], (rows, qcols))
+            qb_ref[f * qcols:(f + 1) * qcols].astype(jnp.float32).reshape(1, -1), (rows, qcols))
         acc[f, :, qcols:cols] = jnp.broadcast_to(
-            small_ref[:, kvb_at + f * kvcols:kvb_at + (f + 1) * kvcols], (rows, kvcols))
+            kvb_ref[f * kvcols:(f + 1) * kvcols].astype(jnp.float32).reshape(1, -1), (rows, kvcols))
     each(slots(PIECE, [VIA_X, VIA_Y], 0) + slots(PIECE, [OWN], 1))
     share([VIA_X, VIA_Y], 0)
     share([OWN], 1)
 
-    seg_row = small_ref[:, seg_at:seg_at + rows]
+    seg_row = seg_ref[...].astype(jnp.float32).reshape(1, -1)
     for b in range(rows // BLOCK):
         at = slice(b * BLOCK, (b + 1) * BLOCK)
         mine = jnp.transpose(jnp.broadcast_to(seg_row[:, at], (BLOCK, BLOCK)))[:, 0:1]
@@ -289,26 +288,29 @@
     far_first = half_heads - near_first
 
     each(slots(PIECE, [OWN], 2) + slots(PIECE, [DIAG], 0), shards(0, OWN, DIAG))
+    each(slots(LATE, [VIA_X, VIA_Y, DIAG], 0))
     share([DIAG], 0)
     share([OWN], 2)
     each(slots(PIECE, [VIA_X, VIA_Y], 1), shards(0, DIAG, DIAG + 1), shards(1, OWN, VIA_X))
-    each(slots(LATE, [VIA_X, VIA_Y, DIAG], 0))
     each(slots(PIECE, [OWN], 3), shards(2, OWN, VIA_X))
     share([OWN], 3)
+    each(slots(LATE, [VIA_X, VIA_Y, DIAG], 1))
     each(slots(PIECE, [VIA_X, VIA_Y], 2), shards(3, OWN, VIA_X))
-    each(slots(LATE, [VIA_X, VIA_Y, DIAG], 1))
+    each(slots(LATE, [VIA_X, VIA_Y, DIAG], 2))
+    share([VIA_X, VIA_Y], 2)
     each(slots(PIECE, [DIAG], 1))
     share([VIA_X, VIA_Y, DIAG], 1)
-    each(slots(LATE, [VIA_X, VIA_Y, DIAG], 2))
     each(slots(PIECE, [VIA_X, VIA_Y], 3), shards(1, VIA_X, DIAG + 1))
+    run_all(*shards(2, VIA_X, DIAG))
     each(slots(PIECE, [DIAG], 2))
-    share([VIA_X, VIA_Y, DIAG], 2)
+    share([DIAG], 2)
     each(slots(LATE, [VIA_X, VIA_Y, DIAG], 3))
     share([VIA_X, VIA_Y], 3)
-    run_all(*shards(2, VIA_X, DIAG + 1))
+    run_all(*shards(2, DIAG, DIAG + 1))
     run_all(half_heads, lambda i: attend_group(near_first + i))
-    each(slots(PIECE, [DIAG], 3), shards(3, VIA_X, DIAG))
+    each(slots(PIECE, [DIAG], 3))
     share([DIAG], 3)
+    run_all(*shards(3, VIA_X, DIAG))
     run_all(*shards(3, DIAG, DIAG + 1))
     run_all(half_heads, lambda i: attend_group(far_first + i))
 
@@ -350,12 +352,10 @@
     vmem = pl.BlockSpec(memory_space=pltpu.VMEM)
     hbm = pl.BlockSpec(memory_space=pl.ANY)
     bf16, f32 = jnp.bfloat16, jnp.float32
-    small = jnp.concatenate(
-        [part.astype(f32) for part in (norm_gain, q_bias, kv_bias, segments)]).reshape(1, -1)
     return pl.pallas_call(
         functools.partial(gather_project_kernel, ndp, nz, pieces, late),
         out_shape=jax.ShapeDtypeStruct((rows, qcols * nz), bf16),
-        in_specs=[hbm, hbm, hbm, vmem],
+        in_specs=[hbm, hbm, hbm] + [vmem] * 4,
         out_specs=vmem,
         scratch_shapes=[
             pltpu.VMEM((ndp, nz, depth, qcols + kvcols), bf16),
@@ -378,7 +378,7 @@
             flops=2 * rows * width * nz * (qcols + kvcols),
             bytes_accessed=2 * rows * width, transcendentals=0),
         name="gather_project_attend",
-    )(hidden, q_weight, kv_weight, small)
+    )(hidden, q_weight, kv_weight, norm_gain, q_bias, kv_bias, segments)
 
 
 def positions_of(segments):

time: 167 us -> 154 us (0.922)
  the two profiles are of different devices: /device:TPU:0 before, /device:TPU:16 now
where the time goes in v5:
time: 154 us
  Pallas kernels  151 us (98%)
  local copies, waits for them, and re-layouts  2.94 us (2%)
    pallas_call x1, Pallas kernels, gather_project(): pl.pallas_call(functools.partial(gather_project_kernel, ndp, nz, pieces,...  151 us

profile of v5, /device:TPU:16, one launch (start us, length us, event | category | flops | bytes accessed | tf_op | source)
XLA Modules:
  0.0 153.9 jit_solution(2950969328505069379)
XLA Ops:
  0.0 151.0 %gather_project_attend.1 = bf16[384,2560]{1,0:T(8,128)(2,1)} custom-call(bf16[384,5120]{1,0:T(8,128)(2,1)} %hidden_ref.1, bf16[640,640]{1,0:T(8,128)(2,1)} %qw_ref.1, bf16[640,256]{1,0:T(8,128)(2,1)} %kvw_ref.1, bf16[5120]{0:T(1024)(128)(2,1)} %gain_ref.1, bf16[2560]{0:T(1024)(128)(2,1)} %qb_ref.1, bf16[1024]{0:T(1024)(128)(2,1)} %kvb_ref.1, s32[384]{0:T(512)} %seg_ref.1), custom_call_target="tpu_custom_call" | custom-call | flops 14092861440 | bytes 3932160 | tf_op jit(solution)/shard_map/gather_project_attend/pallas_call | solution.py:355
  151.0 2.9 %copy.9 = bf16[384,2560]{1,0:T(8,128)(2,1)} copy(bf16[384,2560]{1,0:T(8,128)(2,1)} %gather_project_attend.1) | data formatting | bytes 3932160

commit v6 on v5

--- a/solution.py
+++ b/solution.py
@@ -295,19 +295,41 @@
     each(slots(PIECE, [OWN], 3), shards(2, OWN, VIA_X))
     share([OWN], 3)
     each(slots(LATE, [VIA_X, VIA_Y, DIAG], 1))
-    each(slots(PIECE, [VIA_X, VIA_Y], 2), shards(3, OWN, VIA_X))
+    share([VIA_X, VIA_Y], 1)
+    each(slots(PIECE, [VIA_X, VIA_Y], 2), shards(3, OWN, VIA_X), shards(1, VIA_X, DIAG))
     each(slots(LATE, [VIA_X, VIA_Y, DIAG], 2))
     share([VIA_X, VIA_Y], 2)
+
+    inner = (z > 0) & (z < nz - 1)
+    count, second_hop = shards(2, VIA_X, DIAG)
+
+    @pl.when(inner)
+    def _():
+        run_all(count, second_hop)
+
+    def second_hop_at_end(i):
+        @pl.when(jnp.logical_not(inner))
+        def _():
+            second_hop(i)
+
     each(slots(PIECE, [DIAG], 1))
-    share([VIA_X, VIA_Y, DIAG], 1)
-    each(slots(PIECE, [VIA_X, VIA_Y], 3), shards(1, VIA_X, DIAG + 1))
-    run_all(*shards(2, VIA_X, DIAG))
+    share([DIAG], 1)
+    each(slots(PIECE, [VIA_X, VIA_Y], 3), shards(1, DIAG, DIAG + 1), (count, second_hop_at_end))
+
+    @pl.when(inner)
+    def _():
+        run_all(half_heads, lambda i: attend_group(near_first + i))
+
     each(slots(PIECE, [DIAG], 2))
     share([DIAG], 2)
     each(slots(LATE, [VIA_X, VIA_Y, DIAG], 3))
     share([VIA_X, VIA_Y], 3)
     run_all(*shards(2, DIAG, DIAG + 1))
-    run_all(half_heads, lambda i: attend_group(near_first + i))
+
+    @pl.when(jnp.logical_not(inner))
+    def _():
+        run_all(half_heads, lambda i: attend_group(near_first + i))
+
     each(slots(PIECE, [DIAG], 3))
     share([DIAG], 3)
     run_all(*shards(3, VIA_X, DIAG))

time: 154 us -> 147 us (0.955)
  the two profiles are of different devices: /device:TPU:16 before, /device:TPU:0 now
where the time goes in v6:
time: 147 us
  Pallas kernels  144 us (98%)
  local copies, waits for them, and re-layouts  2.94 us (2%)
    pallas_call x1, Pallas kernels, gather_project(): pl.pallas_call(functools.partial(gather_project_kernel, ndp, nz, pieces,...  144 us
    unnamed x1, local copies, waits for them, and re-layouts  2.94 us

profile of v6, /device:TPU:0, one launch (start us, length us, event | category | flops | bytes accessed | tf_op | source)
XLA Modules:
  0.0 147.2 jit_solution(14199413594388309774)
XLA Ops:
  0.0 144.3 %gather_project_attend.1 = bf16[384,2560]{1,0:T(8,128)(2,1)} custom-call(bf16[384,5120]{1,0:T(8,128)(2,1)} %hidden_ref.1, bf16[640,640]{1,0:T(8,128)(2,1)} %qw_ref.1, bf16[640,256]{1,0:T(8,128)(2,1)} %kvw_ref.1, bf16[5120]{0:T(1024)(128)(2,1)} %gain_ref.1, bf16[2560]{0:T(1024)(128)(2,1)} %qb_ref.1, bf16[1024]{0:T(1024)(128)(2,1)} %kvb_ref.1, s32[384]{0:T(512)} %seg_ref.1), custom_call_target="tpu_custom_call" | custom-call | flops 14092861440 | bytes 3932160 | tf_op jit(solution)/shard_map/gather_project_attend/pallas_call | solution.py:377
  144.3 2.9 %copy.9 = bf16[384,2560]{1,0:T(8,128)(2,1)} copy(bf16[384,2560]{1,0:T(8,128)(2,1)} %gather_project_attend.1) | data formatting | bytes 3932160

commit v7 on v6

--- a/solution.py
+++ b/solution.py
@@ -337,7 +337,9 @@
     run_all(half_heads, lambda i: attend_group(far_first + i))
 
     def sent(way, plane, count):
-        some = wbuf.at[pl.ds(0, count), 0, pl.ds(0, step), :]
+        total = count * step
+        parts = next(p for p in range(1, ndp + 1) if total % (p * 16) == 0 and total // p <= depth)
+        some = wbuf.at[pl.ds(0, parts), 0, pl.ds(0, total // parts), :]
         pltpu.make_async_copy(some, some, send_sem.at[way, plane]).wait()
 
     def flat(plane, carry):
@@ -370,7 +372,7 @@
     rows, width = hidden.shape
     depth, qcols = q_weight.shape
     kvcols = kv_weight.shape[1]
-    pieces, late = 5, 1
+    pieces, late = 10, 2
     vmem = pl.BlockSpec(memory_space=pltpu.VMEM)
     hbm = pl.BlockSpec(memory_space=pl.ANY)
     bf16, f32 = jnp.bfloat16, jnp.float32

time: 147 us -> 146 us (level)
  no operation moved by 1% of the time
where the time goes in v7:
time: 146 us
  Pallas kernels  143 us (98%)
  local copies, waits for them, and re-layouts  2.94 us (2%)
    pallas_call x1, Pallas kernels, gather_project(): pl.pallas_call(functools.partial(gather_project_kernel, ndp, nz, pieces,...  143 us
    unnamed x1, local copies, waits for them, and re-layouts  2.94 us

profile of v7, /device:TPU:0, one launch (start us, length us, event | category | flops | bytes accessed | tf_op | source)
XLA Modules:
  0.0 146.2 jit_solution(16183717201523816774)
XLA Ops:
  0.0 143.2 %gather_project_attend.1 = bf16[384,2560]{1,0:T(8,128)(2,1)} custom-call(bf16[384,5120]{1,0:T(8,128)(2,1)} %hidden_ref.1, bf16[640,640]{1,0:T(8,128)(2,1)} %qw_ref.1, bf16[640,256]{1,0:T(8,128)(2,1)} %kvw_ref.1, bf16[5120]{0:T(1024)(128)(2,1)} %gain_ref.1, bf16[2560]{0:T(1024)(128)(2,1)} %qb_ref.1, bf16[1024]{0:T(1024)(128)(2,1)} %kvb_ref.1, s32[384]{0:T(512)} %seg_ref.1), custom_call_target="tpu_custom_call" | custom-call | flops 14092861440 | bytes 3932160 | tf_op jit(solution)/shard_map/gather_project_attend/pallas_call | solution.py:379
  143.2 2.9 %copy.9 = bf16[384,2560]{1,0:T(8,128)(2,1)} copy(bf16[384,2560]{1,0:T(8,128)(2,1)} %gather_project_attend.1) | data formatting | bytes 3932160

commit v8 on v7

--- a/solution.py
+++ b/solution.py
@@ -22,7 +22,7 @@
     ndp, nz, pieces, late,
     hidden_ref, qw_ref, kvw_ref, gain_ref, qb_ref, kvb_ref, seg_ref,
     out_ref,
-    wbuf, raw, normed, acc, cos_t, sin_t, mask_t, k_buf, v_buf, local_sem, send_sem, share_sem, recv_sem,
+    wbuf, raw, normed, acc, cos_t, sin_t, mask_t, k_buf, v_buf, local_sem, out_sem, send_sem, share_sem, recv_sem,
 ):
     rows, width = raw.shape
     depth, qcols = qw_ref.shape
@@ -256,6 +256,10 @@
         v_buf[g] = acc[key_planes + g // per_plane, :, lanes].astype(jnp.bfloat16)
 
     scale = HEAD_DIM ** (-0.5) * 1.4426950408889634
+
+    def result(g):
+        lanes = pl.ds(pl.multiple_of(g * group * HEAD_DIM, HEAD_DIM), group * HEAD_DIM)
+        return pltpu.make_async_copy(raw.at[:, lanes], out_ref.at[:, lanes], out_sem.at[g])
 
     def attend_group(g):
         prepare(g)
@@ -281,7 +285,8 @@
             c = jnp.dot(p, v_buf[g, 0:seen, :], preferred_element_type=jnp.float32)
             for h in range(group):
                 lanes = pl.ds(pl.multiple_of((g * group + h) * HEAD_DIM, HEAD_DIM), HEAD_DIM)
-                out_ref[at, lanes] = c[h * BLOCK:(h + 1) * BLOCK].astype(out_ref.dtype)
+                raw[at, lanes] = c[h * BLOCK:(h + 1) * BLOCK].astype(raw.dtype)
+        result(g).start()
 
     half_heads = KV_HEADS // 2
     near_first = (z // (nz // 2)) * half_heads
@@ -364,6 +369,7 @@
         return carry
 
     lax.fori_loop(0, nz, flat, 0)
+    run_all(KV_HEADS, lambda g: result(g).wait())
     lane_shards = wbuf.at[pl.ds(0, ndp // 2)]
     pltpu.make_async_copy(lane_shards, lane_shards, share_sem).wait()
 
@@ -380,7 +386,7 @@
         functools.partial(gather_project_kernel, ndp, nz, pieces, late),
         out_shape=jax.ShapeDtypeStruct((rows, qcols * nz), bf16),
         in_specs=[hbm, hbm, hbm] + [vmem] * 4,
-        out_specs=vmem,
+        out_specs=hbm,
         scratch_shapes=[
             pltpu.VMEM((ndp, nz, depth, qcols + kvcols), bf16),
             pltpu.VMEM((rows, width), bf16),
@@ -392,12 +398,13 @@
             pltpu.VMEM((KV_HEADS, rows, HEAD_DIM), bf16),
             pltpu.VMEM((KV_HEADS, rows, HEAD_DIM), bf16),
             pltpu.SemaphoreType.DMA((3,)),
+            pltpu.SemaphoreType.DMA((KV_HEADS,)),
             pltpu.SemaphoreType.DMA((4, nz)),
             pltpu.SemaphoreType.DMA(()),
             pltpu.SemaphoreType.DMA((ndp, nz, pieces)),
         ],
         compiler_params=pltpu.CompilerParams(
-            collective_id=0, has_side_effects=True, vmem_limit_bytes=60 * 2**20),
+            collective_id=0, has_side_effects=True, vmem_limit_bytes=57 * 2**20),
         cost_estimate=pl.CostEstimate(
             flops=2 * rows * width * nz * (qcols + kvcols),
             bytes_accessed=2 * rows * width, transcendentals=0),

time: 146 us -> 146 us (level)
  no operation moved by 1% of the time
where the time goes in v8:
time: 146 us
  Pallas kernels  143 us (98%)
  local copies, waits for them, and re-layouts  2.94 us (2%)
    pallas_call x1, Pallas kernels, gather_project(): pl.pallas_call(functools.partial(gather_project_kernel, ndp, nz, pieces,...  143 us
    unnamed x1, local copies, waits for them, and re-layouts  2.94 us

profile of v8, /device:TPU:0, one launch (start us, length us, event | category | flops | bytes accessed | tf_op | source)
XLA Modules:
  0.0 145.7 jit_solution(14485480171050402484)
XLA Ops:
  0.0 142.8 %gather_project_attend.1 = bf16[384,2560]{1,0:T(8,128)(2,1)} custom-call(bf16[384,5120]{1,0:T(8,128)(2,1)} %hidden_ref.1, bf16[640,640]{1,0:T(8,128)(2,1)} %qw_ref.1, bf16[640,256]{1,0:T(8,128)(2,1)} %kvw_ref.1, bf16[5120]{0:T(1024)(128)(2,1)} %gain_ref.1, bf16[2560]{0:T(1024)(128)(2,1)} %qb_ref.1, bf16[1024]{0:T(1024)(128)(2,1)} %kvb_ref.1, s32[384]{0:T(512)} %seg_ref.1), custom_call_target="tpu_custom_call" | custom-call | flops 14092861440 | bytes 3932160 | tf_op jit(solution)/shard_map/gather_project_attend/pallas_call | solution.py:385
  142.8 2.9 %copy.9 = bf16[384,2560]{1,0:T(8,128)(2,1)} copy(bf16[384,2560]{1,0:T(8,128)(2,1)} %gather_project_attend.1) | data formatting | bytes 3932160
